TPU v7x, 256 devices: a whole 4x4x8 slice. The times are simulated.
256 devices in a mesh: dp: 32 (over y, z), tensor: 8 (over x, core).
Axes of the slice: x: 4, y: 4, z: 8, core: 2. Of those that a mesh axis runs over, the one named last changes fastest.
Arguments:
- pixels: bfloat16 [32, 256, 128], P(None, ('dp', 'tensor')), may hold values from -6 to 6
- counts: int32 [32], replicated, may hold values from 1 to 8, as said below
- var_ids: int32 [32, 8], replicated, may hold values from 0 to 47, as said below
- destination: int32 [32], replicated, may hold values from 0 to 31, each once
- embed_weight: bfloat16 [48, 16, 4096], P(None, None, 'tensor'), may hold values from -1.5 to 1.5
- var_embed: bfloat16 [48, 4096], P(None, 'tensor'), may hold values from -4 to 4
- agg_query: bfloat16 [4096], P('tensor'), may hold values from -200 to 200
- ln_gain: bfloat16 [1, 4096], P(None, 'tensor'), may hold values from 0.25 to 1.75
- fc_up: bfloat16 [4096, 8192], P(None, 'tensor'), may hold values from -0.09375 to 0.09375
- fc_down: bfloat16 [4096, 8192], P('dp', 'tensor'), may hold values from -0.0625 to 0.0625
- cotangent: bfloat16 [32, 256, 4096], P('dp', None, 'tensor'), may hold values from -6 to 6
Outputs:
- mixed: bfloat16 [32, 256, 4096], P('dp', None, 'tensor')
- grad_embed: float32 [48, 16, 4096], P(None, None, 'tensor')
- grad_var: float32 [48, 4096], P(None, 'tensor')
- grad_query: float32 [4096], P('tensor')
Inputs may be any that keep to these rules, and one draw needn't show every extreme that they name: `counts`: some sample has 8 live variables in every draw. `var_ids`: the ids of one sample's slots are distinct. `destination`: each rank is named once.
All inputs are finite; a program needn't handle non-finite values.
Results may differ from a plain program's by a relative error of at most 0.017.
The roundings to bfloat16 on the way count: a program that leaves them out, or rounds other values in their place, can miss the bound.
Values may be sent and summed in bfloat16 or wider, within the bound.
No kernel may reach another device: no remote copies, remote signals or barrier semaphores. Data moves between devices by JAX's collectives and lax.ppermute only.
A program may use at most 128 MiB of HBM per device.

v0:
```python
import functools

import jax
import jax.numpy as jnp
from jax import lax
from jax.experimental import pallas as pl
from jax.experimental.pallas import tpu as pltpu
from jax.sharding import Mesh, PartitionSpec as P

HEAD = 128
VMAX = 8
PP = 16
NVAR = 48
D = 4096
FF = 8192
NP = 256
W = 512
HID = 1024
EXT = NP + 16
BF = jnp.bfloat16
F32 = jnp.float32
NT = (((1,), (1,)), ((), ()))
VM = pl.BlockSpec(memory_space=pltpu.VMEM)
SM = pl.BlockSpec(memory_space=pltpu.SMEM)
NX, NY, NZ, NC = 4, 4, 8, 2
BIG = 16


def params(mib):
    return pltpu.CompilerParams(vmem_limit_bytes=mib << 20)


def call(kernel, outs, n_smem, n_vmem, scratch=(), mib=BIG, flops=0, nbytes=0, name=None):
    single = not isinstance(outs, (list, tuple))
    return pl.pallas_call(
        kernel,
        out_shape=outs if single else tuple(outs),
        in_specs=[SM] * n_smem + [VM] * n_vmem,
        out_specs=VM if single else tuple([VM] * len(outs)),
        scratch_shapes=list(scratch),
        compiler_params=params(mib),
        cost_estimate=pl.CostEstimate(flops=flops, bytes_accessed=nbytes, transcendentals=0),
        name=name,
    )


def sds(shape, dtype):
    return jax.ShapeDtypeStruct(shape, dtype)


def hbm(a):
    return pltpu.with_memory_space_constraint(a, pltpu.HBM)


def send(a, axis, k):
    n = {"x": NX, "y": NY, "z": NZ, "c": NC}[axis]
    return lax.ppermute(a, axis, [(i, (i + k) % n) for i in range(n)])


def around(a, axis):
    n = {"x": NX, "y": NY, "z": NZ}[axis]
    steps = [(2 * i + k, 2 * ((i + 1 - 2 * k) % n) + k) for i in range(n) for k in range(NC)]
    return lax.ppermute(a, (axis, "c"), steps)


def dot(a, b, dims=(((1,), (0,)), ((), ()))):
    return lax.dot_general(a, b, dims, preferred_element_type=F32)


def lane_group(shape):
    return lax.broadcasted_iota(jnp.int32, shape, 1) // 16


def head_mask(dtype):
    row = lax.broadcasted_iota(jnp.int32, (128, W), 0)
    col = lax.broadcasted_iota(jnp.int32, (128, W), 1)
    return jnp.where(row % 16 == col // HEAD, 1.0, 0.0).astype(dtype)


def over_slots(op, a):
    for shift in (16, 32, 64):
        a = op(a, pltpu.roll(a, shift, 1))
    return a


def find(destination, rank):
    return lax.fori_loop(0, NY * NZ, lambda i, s: jnp.where(destination[i] == rank, i, s), 0)


def fwd_kernel(info, destination, counts, var_ids, xa_ref, xb_ref, ew_ref, ve_ref, q_ref, gain_ref,
               agg_ref, emb_ref, attn_ref, x_ref, wblk, wsem):
    copies = []
    sample = find(destination, info[0] * NZ + info[1])
    count = counts[sample]
    ids = [var_ids[sample * VMAX + j] for j in range(VMAX)]
    for j in range(VMAX):
        copies.append(pltpu.make_async_copy(ew_ref.at[ids[j]], wblk.at[j, pl.ds(16 * j, 16), :], wsem.at[j]))
    zero = jnp.zeros((16, W), BF)
    for j in range(VMAX):
        for k in range(VMAX):
            if k != j:
                wblk[j, 16 * k:16 * (k + 1), :] = zero
    for cp in copies:
        cp.start()
    col = lax.broadcasted_iota(jnp.int32, (1, NP), 1)
    device = jnp.zeros((1, NP), jnp.int32)
    for k in range(8):
        chip, core = (info[2] + (0, 3, 1, 2)[k % 4]) % 4, (info[3] + k // 4) % 2
        device = jnp.where(col // 32 == k, 2 * chip + core, device)
    row = lax.broadcasted_iota(jnp.int32, (NP, NP), 0)
    order = jnp.where(row == 8 * (col % 32) + device, 1.0, 0.0).astype(BF)
    pieces = jnp.concatenate([r[k] for r in (xa_ref, xb_ref) for k in range(4)], axis=0)
    x_ref[...] = dot(order, pieces).astype(BF)
    at_slot = lax.broadcasted_iota(jnp.int32, (16, NVAR), 0)
    at_var = lax.broadcasted_iota(jnp.int32, (16, NVAR), 1)
    onehot = jnp.zeros((16, NVAR), F32)
    for j in range(VMAX):
        onehot = jnp.where((at_slot == j) & (at_var == ids[j]), 1.0, onehot)
    bias = dot(onehot.astype(BF), ve_ref[...])
    expand = head_mask(BF)
    qmat = (expand.astype(F32) * q_ref[...].astype(F32)).astype(BF)
    for cp in copies:
        cp.wait()
    rows = 128
    group = lane_group((rows, 128))
    for r in range(NP // rows):
        at = slice(r * rows, (r + 1) * rows)
        x = x_ref[at, :]
        scores = jnp.zeros((rows, 128), F32)
        for j in range(VMAX):
            e = (dot(x, wblk[j]) + bias[j:j + 1, :]).astype(BF)
            emb_ref[j, at, :] = e
            scores = jnp.where(group == j, dot(e, qmat, NT), scores)
        scores = scores * (HEAD ** -0.5)
        scores = jnp.where(group < count, scores, -jnp.inf)
        top = over_slots(jnp.maximum, scores)
        raised = jnp.exp(scores - top)
        attn = raised / over_slots(jnp.add, raised)
        attn_ref[at, :] = attn
        attn_b = attn.astype(BF)
        total = jnp.zeros((rows, W), F32)
        for j in range(VMAX):
            wide = dot(jnp.where(group == j, attn_b, jnp.zeros_like(attn_b)), expand)
            total = total + wide * emb_ref[j, at, :].astype(F32)
        agg_ref[at, :] = total.astype(BF)
    agg_ref[NP:EXT, :] = jnp.broadcast_to(gain_ref[...], (16, W))


def attention_forward(info, routing, xs, ew, ve, q, gain):
    return pl.pallas_call(
        fwd_kernel,
        out_shape=(sds((EXT, W), BF), sds((VMAX, NP, W), BF), sds((NP, 128), F32), sds((NP, 128), BF)),
        in_specs=[SM] * 4 + [VM, VM, pl.BlockSpec(memory_space=pl.ANY), VM, VM, VM],
        out_specs=(VM, VM, VM, VM),
        scratch_shapes=[pltpu.VMEM((VMAX, 128, W), BF), pltpu.SemaphoreType.DMA((VMAX,))],
        compiler_params=params(BIG),
        cost_estimate=pl.CostEstimate(flops=2 * 3 * 8 * 256 * 128 * 512, bytes_accessed=4 << 20, transcendentals=0),
        name="attn_fwd",
    )(info, *routing, *xs, ew, ve, q, gain)


def tensor_gather(a):
    first = around(a, "x")
    other = send(a, "c", 1)
    second = around(other, "x")
    far = around(first, "x")
    return a, other, first, second, far, send(first, "c", 1), send(second, "c", 1), send(far, "c", 1)


def blocks_of(info, refs):
    x, c = info[2], info[3]
    d = 1 - 2 * c
    back, fore, opposite = (x + 4 - d) % 4, (x + 4 + d) % 4, (x + 2) % 4
    place = ((x, c), (x, 1 - c), (back, c), (back, 1 - c), (opposite, c), (fore, 1 - c), (fore, c), (opposite, 1 - c))
    return [(chip, core, ref) for (chip, core), ref in zip(place, refs)]


def up_kernel(info, *refs):
    pieces, up_ref = refs[:8], refs[8]
    pre_ref, dg_ref, hid_ref, u_ref, st_ref, nrm = refs[9:]

    @pl.when(pl.program_id(0) == 0)
    def _():
        blocks = [(2 * chip + core, p) for chip, core, p in blocks_of(info, pieces)]
        for r in range(4):
            lo, hi = 64 * r, 64 * r + 64
            total = jnp.zeros((64, W), F32)
            for _, p in blocks:
                total = total + p[lo:hi, :].astype(F32)
            mean = jnp.sum(total, axis=1, keepdims=True) * (1.0 / D)
            total = jnp.zeros((64, W), F32)
            for _, p in blocks:
                d = p[lo:hi, :].astype(F32) - mean
                total = total + d * d
            inv = lax.rsqrt(jnp.sum(total, axis=1, keepdims=True) * (1.0 / D) + 1e-05)
            st_ref[0, lo:hi, :] = jnp.broadcast_to(mean, (64, 128))
            st_ref[1, lo:hi, :] = jnp.broadcast_to(inv, (64, 128))
            for b, p in blocks:
                gain = p[NP:EXT, :][0:1, :].astype(F32)
                col = pl.ds(pl.multiple_of(b * W, W), W)
                nrm[lo:hi, col] = ((p[lo:hi, :].astype(F32) - mean) * inv * gain).astype(BF)
        for b, p in blocks:
            nrm[NP:EXT, pl.ds(pl.multiple_of(b * W, W), W)] = p[NP:EXT, :]

    acc = dot(nrm[...], up_ref[...])
    x = acc[:NP]
    c = 0.7978845608028654
    th = jnp.tanh(c * (x + 0.044715 * (x * x * x)))
    pre_ref[...] = x
    hid_ref[...] = (0.5 * x * (1.0 + th)).astype(BF)
    dg_ref[...] = 0.5 * (1.0 + th) + 0.5 * x * (1.0 - th * th) * (c * (1.0 + 3 * 0.044715 * (x * x)))
    u_ref[...] = acc[NP:NP + 8]


def up_call(info, pieces, fc_up):
    n = 4
    w = HID // n
    whole = [pl.BlockSpec(p.shape, lambda i: (0, 0)) for p in pieces]
    return pl.pallas_call(
        up_kernel,
        grid=(n,),
        out_shape=(sds((NP, HID), F32), sds((NP, HID), F32), sds((NP, HID), BF), sds((8, HID), F32), sds((2, NP, 128), F32)),
        in_specs=[SM] + whole + [pl.BlockSpec((D, w), lambda i: (0, i))],
        out_specs=(
            pl.BlockSpec((NP, w), lambda i: (0, i)), pl.BlockSpec((NP, w), lambda i: (0, i)),
            pl.BlockSpec((NP, w), lambda i: (0, i)), pl.BlockSpec((8, w), lambda i: (0, i)),
            pl.BlockSpec((2, NP, 128), lambda i: (0, 0, 0)),
        ),
        scratch_shapes=[pltpu.VMEM((EXT, D), BF)],
        compiler_params=params(BIG),
        cost_estimate=pl.CostEstimate(flops=2 * EXT * D * HID, bytes_accessed=16 << 20, transcendentals=0),
        name="ln_up",
    )(info, *map(hbm, pieces), hbm(fc_up))


def split3(row):
    hi = row.astype(BF).astype(F32)
    mid = (row - hi).astype(BF).astype(F32)
    return hi, mid, row - hi - mid


def ride(row):
    hi, mid, low = split3(row)
    at = lax.broadcasted_iota(jnp.int32, (16, W), 0)
    tile = jnp.where(at == 0, hi, jnp.where(at == 1, mid, jnp.where(at == 2, low, 0.0)))
    return tile.astype(BF)


def unride(tile):
    return jnp.sum(tile.astype(F32), axis=0, keepdims=True)


def join_kernel(info, *refs):
    pieces, out = refs[:8], refs[8]
    for chip, core, p in blocks_of(info, pieces):
        out[:, pl.ds(pl.multiple_of((2 * chip + core) * W, W), W)] = p[...]


def join(info, pieces):
    return call(join_kernel, sds((NP, D), BF), 1, 8, mib=BIG, nbytes=4 << 20, name="join")(info, *map(hbm, pieces))


def gh_kernel(g, down_ref, pre_ref, dg_ref, u_ref, gp_ref, s_ref, tot):
    i = pl.program_id(0)

    @pl.when(i == 0)
    def _():
        tot[...] = jnp.zeros_like(tot)

    gh = dot(g[...], down_ref[...])
    gp = (gh * dg_ref[...]).astype(BF)
    gp_ref[...] = gp
    gpf = gp.astype(F32)
    a = gpf * u_ref[0:1, :]
    b = gpf * pre_ref[...]
    tot[0] += a[:, :128] + a[:, 128:]
    tot[1] += b[:, :128] + b[:, 128:]

    @pl.when(i == pl.num_programs(0) - 1)
    def _():
        s_ref[...] = ride(sums_row(tot[0], tot[1]))


def grad_pre(g, down, pre, dg, u):
    n = 4
    w = HID // n

    def col(r):
        return pl.BlockSpec((r, w), lambda i: (0, i))

    return pl.pallas_call(
        gh_kernel,
        grid=(n,),
        out_shape=(sds((NP, HID), BF), sds((16, W), BF)),
        in_specs=[VM, col(D), col(NP), col(NP), col(8)],
        out_specs=(col(NP), pl.BlockSpec((16, W), lambda i: (0, 0))),
        scratch_shapes=[pltpu.VMEM((2, NP, 128), F32)],
        compiler_params=params(BIG),
        cost_estimate=pl.CostEstimate(flops=2 * NP * D * HID, bytes_accessed=12 << 20, transcendentals=0),
        name="grad_pre",
    )(g, hbm(down), hbm(pre), hbm(dg), u)


def sums_row(a, b):
    rows = []
    for t in (a, b):
        s = jnp.broadcast_to(jnp.sum(t, axis=1, keepdims=True), (NP, 128))
        rows.append(jnp.transpose(s)[0:1, :])
    return jnp.concatenate(rows, axis=1)


def keep_kernel(src, dst, sem):
    copy = pltpu.make_async_copy(src, dst, sem)
    copy.start()
    copy.wait()


def keep(a):
    return pl.pallas_call(
        keep_kernel,
        out_shape=pltpu.VMEM(a.shape, a.dtype),
        in_specs=[pl.BlockSpec(memory_space=pltpu.HBM)],
        out_specs=pl.BlockSpec(memory_space=pltpu.VMEM),
        scratch_shapes=[pltpu.SemaphoreType.DMA],
        compiler_params=params(12),
        cost_estimate=pl.CostEstimate(flops=0, bytes_accessed=2 * a.size * 2, transcendentals=0),
        name="keep",
    )(a)


def nt_kernel(steps, other, kept, with_sums, first_add, stacked, info, lhs_ref, rhs_ref, *refs):
    refs = list(refs)
    s_ref = refs.pop(0) if with_sums else None
    add_ref = refs.pop(0) if first_add is not None else None
    core = 1 - info[3] if other else info[3]
    n = len(steps)
    rows = [pl.ds(pl.multiple_of((2 * ((info[2] + k) % NX) + core) * W, W), W) for k in steps]
    if not kept:
        buf, sem = refs[-2:]
        copies = [pltpu.make_async_copy(rhs_ref.at[rows[i], :], buf.at[i], sem.at[i]) for i in range(n)]
        for cp in copies:
            cp.start()
    for i in range(n):
        if not kept:
            copies[i].wait()
        out = refs[0].at[i] if stacked else refs[i]
        acc = dot(lhs_ref[...], rhs_ref[rows[i], :] if kept else buf[i], NT)
        if first_add is not None:
            acc = acc + add_ref[first_add + i, :NP, :].astype(F32)
        out[:NP, :] = acc.astype(BF)
        if with_sums:
            if first_add is not None:
                out[NP:, :] = ride(unride(s_ref[...]) + unride(add_ref[first_add + i, NP:, :]))
            else:
                out[NP:, :] = s_ref[...]


def nt_call(steps, other, kept, info, lhs, rhs, sums=None, add=None, first_add=None, stacked=False, name=None):
    n = len(steps)
    rows = EXT if sums is not None else NP
    args = [info, lhs, rhs if kept else hbm(rhs)]
    in_specs = [SM, VM, VM if kept else pl.BlockSpec(memory_space=pltpu.HBM)]
    for extra in (sums, add):
        if extra is not None:
            args.append(extra)
            in_specs.append(VM)
    return pl.pallas_call(
        functools.partial(nt_kernel, steps, other, kept, sums is not None, first_add, stacked),
        in_specs=in_specs,
        out_specs=VM if stacked else tuple([VM] * n),
        out_shape=sds((n, rows, W), BF) if stacked else tuple([sds((rows, W), BF)] * n),
        scratch_shapes=[] if kept else [pltpu.VMEM((n, W, HID), BF), pltpu.SemaphoreType.DMA((n,))],
        compiler_params=params(BIG),
        cost_estimate=pl.CostEstimate(flops=2 * NP * HID * W * n, bytes_accessed=n << 20, transcendentals=0),
        name=name,
    )(*args)


def half_kernel(a_ref, b_ref, out_ref):
    out_ref[:NP, :] = a_ref[:NP, :].astype(F32) + b_ref[:NP, :].astype(F32)
    if a_ref.shape[0] > NP:
        at = lax.broadcasted_iota(jnp.int32, (16, W), 0)
        out_ref[NP:, :] = jnp.where(at == 0, unride(a_ref[NP:, :]) + unride(b_ref[NP:, :]), 0.0)


def tensor_scatter(info, lhs, rhs, sums, name, kept):
    o = send(nt_call((2, 1, 3, 0), True, kept, info, lhs, rhs, sums, stacked=True, name=name + "_o"), "c", 1)
    far, = nt_call((2,), False, kept, info, lhs, rhs, sums, o, 0, name=name + "_f")
    lhs, far = lax.optimization_barrier((lhs, far))
    far = send(far, "x", 2)
    ahead, behind, own = nt_call((1, 3, 0), False, kept, info, lhs, rhs, sums, o, 1, name=name + "_n")
    return call(half_kernel, sds(own.shape, F32), 0, 2, mib=BIG, nbytes=1 << 20, name=name + "_p")(own, far), send(
        ahead, "x", 1), send(behind, "x", -1)


def rows_kernel(x_ref, out_ref):
    row = lax.broadcasted_iota(jnp.int32, (256, 128), 0)
    col = lax.broadcasted_iota(jnp.int32, (256, 128), 1)
    pixel = 16 * (row // 32) + 2 * (row % 32 // 4) + row % 4
    chosen = jnp.where((col == pixel) & (row % 4 < 2), 1.0, 0.0).astype(BF)
    got = dot(chosen, x_ref[...], NT)
    at = lax.broadcasted_iota(jnp.int32, (256, NP), 0)
    out_ref[...] = jnp.where(at % 4 < 2, got, 1.0).astype(BF)


def bwd_kernel(own_ref, p1_ref, p2_ref, agg_ref, st_ref, gain_ref, g_ref, emb_ref, attn_ref, x_ref, q_ref,
               *rest):
    out_ref, acc, gq = rest
    parts = (own_ref, p1_ref, p2_ref)
    expand = head_mask(BF)
    scale = HEAD ** -0.5
    qrow = q_ref[...].astype(F32) * scale
    gain = gain_ref[...].astype(F32)
    sums = sum(unride(p[NP:, :]) for p in parts)
    cols = []
    for k in range(2):
        row = sums[:, k * NP:(k + 1) * NP] * (1.0 / D)
        cols.append(jnp.transpose(jnp.broadcast_to(row, (128, NP))))
    expand2 = jnp.concatenate([expand, expand], axis=0)
    rows = NP
    group = lane_group((rows, 128))
    group2 = lax.broadcasted_iota(jnp.int32, (rows, 256), 1) % 128 // 16
    for r in range(NP // rows):
        at = slice(r * rows, (r + 1) * rows)
        mean, inv = st_ref[0, at, 0:1], st_ref[1, at, 0:1]
        xh = (agg_ref[at, :].astype(F32) - mean) * inv
        gs = sum(p[at, :].astype(F32) for p in parts) * gain
        ga = g_ref[at, :].astype(F32) + inv * (gs - cols[0][at, 0:1] - xh * cols[1][at, 0:1])
        gab = ga.astype(BF).astype(F32)
        gattn = jnp.zeros((rows, 128), F32)
        for j in range(VMAX):
            prod = gab * emb_ref[j, at, :].astype(F32)
            hi = prod.astype(BF)
            low = (prod - hi.astype(F32)).astype(BF)
            both = dot(hi, expand, NT) + dot(low, expand, NT)
            gattn = jnp.where(group == j, both, gattn)
        attn = attn_ref[at, :]
        gscore = attn * (gattn - over_slots(jnp.add, attn * gattn))
        ahi = attn.astype(BF)
        alow = (attn - ahi.astype(F32)).astype(BF)
        shi = gscore.astype(BF)
        slow = (gscore - shi.astype(F32)).astype(BF)
        a2 = jnp.concatenate([ahi, alow], axis=1)
        s2 = jnp.concatenate([shi, slow], axis=1)
        zero = jnp.zeros_like(a2)
        gst = jnp.transpose(shi.astype(F32)).astype(BF)
        for j in range(VMAX):
            pick = group2 == j
            a_w = dot(jnp.where(pick, a2, zero), expand2)
            s_w = dot(jnp.where(pick, s2, zero), expand2)
            ge = (a_w * ga + s_w * qrow).astype(BF)
            mine = slice(16 * j, 16 * j + 16)
            part_q = dot(gst[mine, :], emb_ref[j, at, :])
            gq[mine, :] = part_q if r == 0 else gq[mine, :] + part_q
            got = dot(x_ref[32 * j:32 * j + 32, at], ge)
            for z in range(NZ):
                to = slice(32 * z + 4 * j, 32 * z + 4 * j + 4)
                if r == 0:
                    acc[to, :] = got[4 * z:4 * z + 4]
                else:
                    acc[to, :] += got[4 * z:4 * z + 4]
    total_q = jnp.sum(gq[...] * expand.astype(F32), axis=0, keepdims=True) * scale
    for z in range(NZ):
        acc[32 * z + 3:32 * z + 4, :] = total_q
        for y in range(NY):
            out_ref[NZ * y + z] = acc[32 * z:32 * z + 32, 128 * y:128 * y + 128].astype(BF)


def attention_backward(gn, agg, st, gain, g, emb, attn, x, q):
    return call(
        bwd_kernel, sds((NY * NZ, 32, 128), BF), 0, 11, [pltpu.VMEM((256, W), F32), pltpu.VMEM((128, W), F32)], mib=BIG,
        flops=2 * 6 * 8 * 256 * 128 * 512, nbytes=5 << 20, name="attn_bwd",
    )(gn[0], *map(hbm, gn[1:]), agg, st, gain, hbm(g), emb, attn, x, q)


def sum_kernel(destination, counts, ids, got_ref, main_ref, rest_ref, acc, bias, pair, query, inverse):
    acc[...] = jnp.zeros_like(acc)
    for i in range(NY * NZ):
        inverse[destination[i]] = i
    total = jnp.zeros((8, 128), F32)
    for rank in range(NY * NZ):
        sample = inverse[rank]
        live = counts[sample]
        data = got_ref[rank].astype(F32)
        total = total + data[0:8]
        for j in range(VMAX):
            v = jnp.where(j < live, ids[sample * VMAX + j], NVAR)
            acc[v, 0:4, :] += data[4 * j:4 * j + 4]
    query[...] = total
    for v in range(NVAR):
        pair[2 * v:2 * v + 2, :] = acc[v, 0:2, :]
        bias[v:v + 1, :] = acc[v, 2:3, :]
    for z in range(NZ):
        main_ref[z] = pair[...].astype(BF)
    rest_ref[0:48, :] = bias[...].astype(BF)
    rest_ref[48:64, :] = jnp.broadcast_to(query[3:4, :], (16, 128)).astype(BF)


def spread_kernel(info, *refs):
    pieces = refs[0:4]
    ge_ref, gv_ref, gq_ref, pair = refs[4:]
    for k, piece in enumerate(pieces):
        col = pl.ds(pl.multiple_of((info[0] + (0, 3, 1, 2)[k]) % NY * 128, 128), 128)
        for z in range(NZ):
            pair[...] = piece[96 * z:96 * z + 96, :].astype(F32)
            for v in range(NVAR):
                ge_ref[v, 2 * z:2 * z + 2, col] = pair[2 * v:2 * v + 2, :]
        gv_ref[:, col] = piece[768:816, :].astype(F32)
        gq_ref[:, col] = piece[816:832, :].astype(F32)[0:1]


def gradient_exchange(info, routing, outs):
    got = lax.all_to_all(outs, ("y", "z"), 0, 0, tiled=True)
    main, rest = call(
        sum_kernel, (sds((NZ, 96, 128), BF), sds((64, 128), BF)), 3, 1,
        [pltpu.VMEM((NVAR + 1, 8, 128), F32), pltpu.VMEM((NVAR, 128), F32), pltpu.VMEM((96, 128), F32),
         pltpu.VMEM((8, 128), F32), pltpu.SMEM((NY * NZ,), jnp.int32)],
        mib=BIG, flops=1 << 20, nbytes=2 << 20, name="slot_sum",
    )(*routing, got)
    main = lax.all_to_all(main, "z", 0, 0, tiled=True)
    both = jnp.concatenate([main.reshape(NZ * 96, 128), rest], axis=0)
    pieces = [both, send(both, "y", 1), send(both, "y", -1), send(both, "y", 2)]
    return call(
        spread_kernel, (sds((NVAR, PP, W), F32), sds((NVAR, W), F32), sds((1, W), F32)), 1, 4,
        [pltpu.VMEM((96, 128), F32)], mib=BIG, flops=1 << 20, nbytes=3 << 20, name="spread",
    )(info, both, *map(hbm, pieces[1:]))


def mix_kernel(agg_ref, own, p1, p2, out_ref):
    total = agg_ref[:NP, :].astype(F32)
    for p in (own, p1, p2):
        total = total + p[...].astype(F32)
    out_ref[0] = total.astype(BF)


def pixel_gather(own):
    mine = jnp.stack([own, send(own, "x", 1), send(own, "x", -1), send(own, "x", 2)])
    return mine, send(mine, "c", 1)


def local(pixels, counts, var_ids, destination, embed_weight, var_embed, agg_query, ln_gain, fc_up, fc_down, cotangent):
    y, z, x, c = (lax.axis_index(a) for a in ("y", "z", "x", "c"))
    info = jnp.stack([y, z, x, c]).astype(jnp.int32)
    routing = destination, counts, var_ids.reshape(-1)
    g_own = cotangent[0]
    down = lax.all_gather(fc_down, ("y", "z"), axis=0, tiled=True)

    to_rank = destination[None, :] == jnp.arange(NY * NZ)[:, None]
    ordered = dot(to_rank.astype(BF), pixels[:, 0, :]).astype(BF)
    mine = lax.all_to_all(ordered, ("y", "z"), 0, 0, tiled=True)
    q, info, mine = lax.optimization_barrier((agg_query.reshape(1, W), info, mine))
    mine, swapped = pixel_gather(mine)

    agg, emb, attn, patches = attention_forward(info, routing, (mine, swapped), embed_weight, var_embed, q, ln_gain)
    pieces = tensor_gather(agg)
    pre, dg, hid, u, st = up_call(info, pieces, fc_up)
    g_late, _ = lax.optimization_barrier((g_own, u))
    g_pieces = tensor_gather(g_late)
    up_src, _ = lax.optimization_barrier((fc_up, g_pieces[4]))
    up_kept = keep(up_src)
    rows = call(rows_kernel, sds((256, NP), BF), 0, 1, mib=BIG, nbytes=1 << 20, name="rows")(patches)
    down, up_kept, g_whole, rows = lax.optimization_barrier((down, up_kept, join(info, g_pieces), rows))
    gp, sums = grad_pre(g_whole, down, pre, dg, u)
    gn = tensor_scatter(info, gp, up_kept, sums, "gn", True)
    mark, _ = lax.optimization_barrier((sums, gn[0]))
    hid, _ = lax.optimization_barrier((hid, send(mark, "c", 1)))
    br = tensor_scatter(info, hid, down, None, "br", False)
    outs = attention_backward(gn, agg, st, ln_gain, g_own, emb, attn, rows, q)
    mixed = call(mix_kernel, sds((1, NP, W), BF), 0, 4, mib=BIG, nbytes=1 << 20, name="mix")(
        agg, br[0], *map(hbm, br[1:]))
    ge, gv, gq = gradient_exchange(info, routing, outs)
    return mixed, ge, gv, gq.reshape(W)


def solution(mesh):
    fine = Mesh(mesh.devices.reshape(NY, NZ, NX, NC), ("y", "z", "x", "c"))
    dp, tensor = ("y", "z"), ("x", "c")
    in_specs = (
        P(None, dp + tensor, None), P(), P(), P(), P(None, None, tensor), P(None, tensor), P(tensor),
        P(None, tensor), P(None, tensor), P(dp, tensor), P(dp, None, tensor),
    )
    out_specs = (P(dp, None, tensor), P(None, None, tensor), P(None, tensor), P(tensor))
    return jax.shard_map(local, mesh=fine, in_specs=in_specs, out_specs=out_specs, check_vma=False)
```

profile of v0, /device:TPU:32, one launch (start us, length us, event | category | flops | bytes accessed | tf_op | source)
XLA Modules:
  0.0 212.7 jit_solution(8885955640031033723)
XLA Ops:
  9.3 11.4 %all-to-all-start = ((bf16[32,1,128]{2,1,0:T(2,128)(2,1)}), bf16[32,1,128]{2,1,0:T(2,128)(2,1)S(1)}, u32[]{:S(2)}, u32[]{:S(2)}) async-start(bf16[32,1,128]{2,1,0:T(2,128)(2,1)} %copy.18), calls=%async_computation | async-start | bytes 32768 | tf_op jit(solution)/shard_map/all_to_all | solution.py:550
  21.5 7.8 %all-to-all-done = bf16[32,1,128]{2,1,0:T(2,128)(2,1)S(1)} async-done(((bf16[32,1,128]{2,1,0:T(2,128)(2,1)}), bf16[32,1,128]{2,1,0:T(2,128)(2,1)S(1)}, u32[]{:S(2)}, u32[]{:S(2)}) %all-to-all-start) | async-done | bytes 8224 | tf_op jit(solution)/shard_map/all_to_all | solution.py:550
  29.2 3.0 %collective-permute-start.2 = (bf16[32,128]{1,0:T(8,128)(2,1)S(1)}, bf16[32,128]{1,0:T(8,128)(2,1)S(1)}, u32[]{:S(2)}, u32[]{:S(2)}) collective-permute-start(bf16[32,128]{1,0:T(8,128)(2,1)S(1)} %bitcast.24), channel_id=1, source_target_pairs={{0,4},{2,6},{4,0},{6,2},{1,5},{3,7},{5,1},{7,3},{8,12},{10,14},{12... | collective-permute-start | bytes 24584 | tf_op jit(solution)/shard_map/ppermute | solution.py:57
  32.3 1.1 collective-permute-start.1
  33.4 0.9 collective-permute-start
  34.4 1.5 collective-permute-done.1
  35.9 2.4 %collective-permute-done = bf16[32,128]{1,0:T(8,128)(2,1)S(1)} collective-permute-done((bf16[32,128]{1,0:T(8,128)(2,1)S(1)}, bf16[32,128]{1,0:T(8,128)(2,1)S(1)}, u32[]{:S(2)}, u32[]{:S(2)}) %collective-permute-start) | collective-permute-done | bytes 8224 | tf_op jit(solution)/shard_map/ppermute | solution.py:57
  40.9 1.1 copy-done.12
  43.5 4.6 %attn_fwd.1 = (bf16[272,512]{1,0:T(8,128)(2,1)S(1)}, bf16[8,256,512]{2,1,0:T(8,128)(2,1)S(1)}, f32[256,128]{1,0:T(8,128)S(1)}, bf16[256,128]{1,0:T(8,128)(2,1)S(1)}) custom-call(s32[4]{0:T(128)S(1)} %pad_add_fusion.info, s32[32]{0:T(128)S(1)} %copy-done.8, s32[32]{0:T(128)S(1)} %copy-done.10, s32[256]{0:T(256)S(1)} %reshape.24.var_ids.ids, ...), custom_call_target="tpu_custom_call" | custom-call | flops 805306368 | bytes 4194304 | tf_op jit(solution)/shard_map/attn_fwd/pallas_call | solution.py:150
  48.1 1.3 copy-done.16
  49.6 7.6 %collective-permute-done.5.refs_2_ = bf16[272,512]{1,0:T(8,128)(2,1)S(1)} collective-permute-done((bf16[272,512]{1,0:T(8,128)(2,1)S(1)}, bf16[272,512]{1,0:T(8,128)(2,1)S(1)}, u32[]{:S(2)}, u32[]{:S(2)}) %collective-permute-start.5) | collective-permute-done | bytes 278560 | tf_op jit(solution)/shard_map/ppermute | solution.py:63
  57.4 7.5 %collective-permute-done.7.refs_4_ = bf16[272,512]{1,0:T(8,128)(2,1)S(1)} collective-permute-done((bf16[272,512]{1,0:T(8,128)(2,1)S(1)}, bf16[272,512]{1,0:T(8,128)(2,1)S(1)}, u32[]{:S(2)}, u32[]{:S(2)}) %collective-permute-start.7) | collective-permute-done | bytes 278560 | tf_op jit(solution)/shard_map/ppermute | solution.py:63
  64.9 3.0 %collective-permute-done.6.refs_3_ = bf16[272,512]{1,0:T(8,128)(2,1)S(1)} collective-permute-done((bf16[272,512]{1,0:T(8,128)(2,1)S(1)}, bf16[272,512]{1,0:T(8,128)(2,1)S(1)}, u32[]{:S(2)}, u32[]{:S(2)}) %collective-permute-start.6) | collective-permute-done | bytes 278560 | tf_op jit(solution)/shard_map/ppermute | solution.py:63
  68.2 1.5 collective-permute-done.9.refs_6_
  70.5 8.6 %ln_up.1 = (f32[256,1024]{1,0:T(8,128)S(1)}, f32[256,1024]{1,0:T(8,128)S(1)}, bf16[256,1024]{1,0:T(8,128)(2,1)S(1)}, f32[8,1024]{1,0:T(8,128)S(1)}, f32[2,256,128]{2,1,0:T(8,128)S(1)}) custom-call(s32[4]{0:T(128)S(1)} %pad_add_fusion.info, bf16[272,512]{1,0:T(8,128)(2,1)} %copy-done.4, bf16[272,512]{1,0:T(8,128)(2,1)} %copy-done.19, ...), custom_call_target="tpu_custom_call" | custom-call | flops 2281701376 | bytes 16777216 | tf_op jit(solution)/shard_map/ln_up/pallas_call | solution.py:219
  79.1 1.0 copy-done.6
  80.1 1.4 collective-permute-done.13.refs_1_
  81.6 6.1 %collective-permute-done.11.refs_2_ = bf16[256,512]{1,0:T(8,128)(2,1)S(1)} collective-permute-done((bf16[256,512]{1,0:T(8,128)(2,1)S(1)}, bf16[256,512]{1,0:T(8,128)(2,1)S(1)}, u32[]{:S(2)}, u32[]{:S(2)}) %collective-permute-start.11) | collective-permute-done | bytes 262176 | tf_op jit(solution)/shard_map/ppermute | solution.py:63
  87.7 2.8 %collective-permute-done.14.refs_3_ = bf16[256,512]{1,0:T(8,128)(2,1)S(1)} collective-permute-done((bf16[256,512]{1,0:T(8,128)(2,1)S(1)}, bf16[256,512]{1,0:T(8,128)(2,1)S(1)}, u32[]{:S(2)}, u32[]{:S(2)}) %collective-permute-start.14) | collective-permute-done | bytes 262176 | tf_op jit(solution)/shard_map/ppermute | solution.py:63
  90.5 4.8 %collective-permute-done.12.refs_4_ = bf16[256,512]{1,0:T(8,128)(2,1)S(1)} collective-permute-done((bf16[256,512]{1,0:T(8,128)(2,1)S(1)}, bf16[256,512]{1,0:T(8,128)(2,1)S(1)}, u32[]{:S(2)}, u32[]{:S(2)}) %collective-permute-start.12) | collective-permute-done | bytes 262176 | tf_op jit(solution)/shard_map/ppermute | solution.py:63
  96.1 3.3 %copy-done.1 = bf16[4096,1024]{1,0:T(8,128)(2,1)} copy-done((bf16[4096,1024]{1,0:T(8,128)(2,1)}, bf16[4096,1024]{1,0:T(8,128)(2,1)S(1)}, u32[]{:S(2)}) %copy-start.1) | copy-done | bytes 8388632
  100.9 1.7 join.1.g
  102.6 7.2 %all-gather.2.cloned.1.call-done.rhs_ref.down_ref = bf16[4096,1024]{1,0:T(8,128)(2,1)} async-done(((bf16[128,1024]{1,0:T(8,128)(2,1)}), bf16[4096,1024]{1,0:T(8,128)(2,1)}) %all-gather.2.cloned.1.call-update) | async-done | bytes 8388624 | tf_op jit(solution)/shard_map/all_gather | solution.py:546
  109.8 6.5 %grad_pre.1 = (bf16[256,1024]{1,0:T(8,128)(2,1)S(1)}, bf16[16,512]{1,0:T(8,128)(2,1)S(1)}) custom-call(bf16[256,4096]{1,0:T(8,128)(2,1)S(1)} %join.1.g, bf16[4096,1024]{1,0:T(8,128)(2,1)} %all-gather.2.cloned.1.call-done.rhs_ref.down_ref, f32[256,1024]{1,0:T(8,128)} %copy-done.6, f32[256,1024]{1,0:T(8,128)} %copy-done.7, f32[8,1024]{1,0:T(8,128)S(1)} %get-tuple-element.44.u_ref), custom_call_target="tpu_custom_call" | custom-call | flops 2147483648 | bytes 12582912 | tf_op jit(solution)/shard_map/grad_pre/pallas_call | solution.py:291
  116.4 1.8 gn_o.1
  118.4 2.7 %collective-permute-done.22.refs_1_ = bf16[4,272,512]{2,1,0:T(8,128)(2,1)S(1)} collective-permute-done((bf16[4,272,512]{2,1,0:T(8,128)(2,1)S(1)}, bf16[4,272,512]{2,1,0:T(8,128)(2,1)S(1)}, u32[]{:S(2)}, u32[]{:S(2)}) %collective-permute-start.22) | collective-permute-done | bytes 1114144 | tf_op jit(solution)/shard_map/ppermute | solution.py:57
  121.1 1.0 gn_f.1
  122.1 1.6 gn_n.1
  123.7 1.5 collective-permute-start.24
  125.3 11.4 %collective-permute-start.25 = (bf16[272,512]{1,0:T(8,128)(2,1)S(1)}, bf16[272,512]{1,0:T(8,128)(2,1)S(1)}, u32[]{:S(2)}, u32[]{:S(2)}) collective-permute-start(bf16[272,512]{1,0:T(8,128)(2,1)S(1)} %get-tuple-element.64), channel_id=1, source_target_pairs={{0,6},{2,0},{4,2},{6,4},{1,7},{3,1},{5,3},{7,5},{8,14},{10,8},{12,... | collective-permute-start | bytes 835592 | tf_op jit(solution)/shard_map/ppermute | solution.py:57
  136.7 1.8 collective-permute-start.23
  138.5 4.7 %br_o.1 = bf16[4,256,512]{2,1,0:T(8,128)(2,1)} custom-call(s32[4]{0:T(128)S(1)} %pad_add_fusion.info, bf16[256,1024]{1,0:T(8,128)(2,1)S(1)} %get-tuple-element.49.lhs_ref, bf16[4096,1024]{1,0:T(8,128)(2,1)} %all-gather.2.cloned.1.call-done.rhs_ref.down_ref), custom_call_target="tpu_custom_call" | custom-call | flops 1073741824 | bytes 4194304 | tf_op jit(solution)/shard_map/br_o/pallas_call | solution.py:367
  143.3 3.3 %collective-permute-done.23.b_ref = bf16[272,512]{1,0:T(8,128)(2,1)S(1)} collective-permute-done((bf16[272,512]{1,0:T(8,128)(2,1)S(1)}, bf16[272,512]{1,0:T(8,128)(2,1)S(1)}, u32[]{:S(2)}, u32[]{:S(2)}) %collective-permute-start.23) | collective-permute-done | bytes 278560 | tf_op jit(solution)/shard_map/ppermute | solution.py:57
  146.6 2.2 %collective-permute-done.25.p2_ref = bf16[272,512]{1,0:T(8,128)(2,1)S(1)} collective-permute-done((bf16[272,512]{1,0:T(8,128)(2,1)S(1)}, bf16[272,512]{1,0:T(8,128)(2,1)S(1)}, u32[]{:S(2)}, u32[]{:S(2)}) %collective-permute-start.25) | collective-permute-done | bytes 278560 | tf_op jit(solution)/shard_map/ppermute | solution.py:57
  149.5 5.6 %attn_bwd.1 = bf16[32,32,128]{2,1,0:T(8,128)(2,1)S(1)} custom-call(f32[272,512]{1,0:T(8,128)S(1)} %gn_p.1.own_ref, bf16[272,512]{1,0:T(8,128)(2,1)} %copy-done.38, bf16[272,512]{1,0:T(8,128)(2,1)} %copy-done.39, bf16[272,512]{1,0:T(8,128)(2,1)S(1)} %copy-done.5, f32[2,256,128]{2,1,0:T(8,128)S(1)} %get-tuple-element.65.st_ref, bf16[1,512]{1,0:T(2,128)(2,1)S(1)} %copy-done.15, ...), custom_call_target="tpu_custom_call" | custom-call | flops 1610612736 | bytes 5242880 | tf_op jit(solution)/shard_map/attn_bwd/pallas_call | solution.py:470
  155.2 18.5 %all_to_all.22.got_ref = bf16[32,32,128]{2,1,0:T(8,128)(2,1)S(1)} all-to-all(bf16[32,32,128]{2,1,0:T(8,128)(2,1)S(1)} %attn_bwd.1), channel_id=1, replica_groups=mesh['y'=4,'z'=8,'x'=4,'c'=2] {'y','z'}, dimensions={0} | all-to-all | bytes 524288 | tf_op jit(solution)/shard_map/all_to_all | solution.py:513
  173.6 2.4 %slot_sum.1 = (bf16[8,96,128]{2,1,0:T(8,128)(2,1)}, bf16[64,128]{1,0:T(8,128)(2,1)S(1)}) custom-call(s32[32]{0:T(128)S(1)} %copy-done.9, s32[32]{0:T(128)S(1)} %copy-done.11, s32[256]{0:T(256)S(1)} %reshape.24.var_ids.ids, bf16[32,32,128]{2,1,0:T(8,128)(2,1)S(1)} %all_to_all.22.got_ref), custom_call_target="tpu_custom_call" | custom-call | flops 1048576 | bytes 2097152 | tf_op jit(solution)/shard_map/slot_sum/pallas_call | solution.py:514
  176.0 3.5 %all-to-all-start.2 = ((bf16[8,96,128]{2,1,0:T(8,128)(2,1)}), bf16[8,96,128]{2,1,0:T(8,128)(2,1)S(1)}, u32[]{:S(2)}, u32[]{:S(2)}) async-start(bf16[8,96,128]{2,1,0:T(8,128)(2,1)} %get-tuple-element.69), calls=%async_computation.2 | async-start | bytes 393216 | tf_op jit(solution)/shard_map/all_to_all | solution.py:520
  179.5 2.3 %br_f.1 = bf16[256,512]{1,0:T(8,128)(2,1)S(1)} custom-call(s32[4]{0:T(128)S(1)} %pad_add_fusion.info, bf16[256,1024]{1,0:T(8,128)(2,1)S(1)} %get-tuple-element.49.lhs_ref, bf16[4096,1024]{1,0:T(8,128)(2,1)} %all-gather.2.cloned.1.call-done.rhs_ref.down_ref, bf16[4,256,512]{2,1,0:T(8,128)(2,1)S(1)} %collective-permute-done.18.refs_0_), custom_call_target="tpu_custom_call" | custom-call | flops 268435456 | bytes 1048576 | tf_op jit(solution)/shard_map/br_f/pallas_call | solution.py:367
  181.9 3.2 %br_n.1 = (bf16[256,512]{1,0:T(8,128)(2,1)S(1)}, bf16[256,512]{1,0:T(8,128)(2,1)S(1)}, bf16[256,512]{1,0:T(8,128)(2,1)S(1)}) custom-call(s32[4]{0:T(128)S(1)} %pad_add_fusion.info, bf16[256,1024]{1,0:T(8,128)(2,1)S(1)} %get-tuple-element.49.lhs_ref, bf16[4096,1024]{1,0:T(8,128)(2,1)} %all-gather.2.cloned.1.call-done.rhs_ref.down_ref, ...), custom_call_target="tpu_custom_call" | custom-call | flops 805306368 | bytes 3145728 | tf_op jit(solution)/shard_map/br_n/pallas_call | solution.py:367
  185.1 4.9 %collective-permute-start.20 = (bf16[256,512]{1,0:T(8,128)(2,1)S(1)}, bf16[256,512]{1,0:T(8,128)(2,1)S(1)}, u32[]{:S(2)}, u32[]{:S(2)}) collective-permute-start(bf16[256,512]{1,0:T(8,128)(2,1)S(1)} %get-tuple-element.52), channel_id=1, source_target_pairs={{0,2},{2,4},{4,6},{6,0},{1,3},{3,5},{5,7},{7,1},{8,10},{10,12},{12... | collective-permute-start | bytes 786440 | tf_op jit(solution)/shard_map/ppermute | solution.py:57
  190.0 1.2 collective-permute-start.21
  191.2 1.6 collective-permute-start.28
  192.9 1.8 collective-permute-start.27
  195.5 1.2 collective-permute-done.21.p2
  197.4 1.8 mix.1
  200.2 1.5 collective-permute-done.26.refs_1_
  202.4 3.3 %spread.1 = (f32[48,16,512]{2,1,0:T(8,128)}, f32[48,512]{1,0:T(8,128)}, f32[1,512]{1,0:T(1,128)}) custom-call(s32[4]{0:T(128)S(1)} %pad_add_fusion.info, bf16[832,128]{1,0:T(8,128)(2,1)S(1)} %pad_maximum_fusion.refs_0_, bf16[832,128]{1,0:T(8,128)(2,1)} %copy-done.37, bf16[832,128]{1,0:T(8,128)(2,1)} %copy-done.36, bf16[832,128]{1,0:T(8,128)(2,1)} %copy-done.35), custom_call_target="tpu_custom_call" | custom-call | flops 1048576 | bytes 3145728 | tf_op jit(solution)/shard_map/spread/pallas_call | solution.py:523
  (125 shorter events, 15.2 us)
Async XLA Ops:
  7.2 102.7 %all-gather.2.cloned.1.call-start = ((), (), s32[]{:S(2)}) async-start(), calls=%async_computation.3 | async-start | bytes 8650752 | tf_op jit(solution)/shard_map/all_gather | solution.py:546
  9.3 19.9 %all-to-all-start = ((bf16[32,1,128]{2,1,0:T(2,128)(2,1)}), bf16[32,1,128]{2,1,0:T(2,128)(2,1)S(1)}, u32[]{:S(2)}, u32[]{:S(2)}) async-start(bf16[32,1,128]{2,1,0:T(2,128)(2,1)} %copy.18), calls=%async_computation | async-start | bytes 32768 | tf_op jit(solution)/shard_map/all_to_all | solution.py:550
  29.2 5.2 %collective-permute-start.2 = (bf16[32,128]{1,0:T(8,128)(2,1)S(1)}, bf16[32,128]{1,0:T(8,128)(2,1)S(1)}, u32[]{:S(2)}, u32[]{:S(2)}) collective-permute-start(bf16[32,128]{1,0:T(8,128)(2,1)S(1)} %bitcast.24), channel_id=1, source_target_pairs={{0,4},{2,6},{4,0},{6,2},{1,5},{3,7},{5,1},{7,3},{8,12},{10,14},{12... | collective-permute-start | bytes 24584 | tf_op jit(solution)/shard_map/ppermute | solution.py:57
  32.3 3.7 %collective-permute-start.1 = (bf16[32,128]{1,0:T(8,128)(2,1)S(1)}, bf16[32,128]{1,0:T(8,128)(2,1)S(1)}, u32[]{:S(2)}, u32[]{:S(2)}) collective-permute-start(bf16[32,128]{1,0:T(8,128)(2,1)S(1)} %bitcast.25), channel_id=1, source_target_pairs={{0,6},{2,0},{4,2},{6,4},{1,7},{3,1},{5,3},{7,5},{8,14},{10,8},{12,... | collective-permute-start | bytes 24584 | tf_op jit(solution)/shard_map/ppermute | solution.py:57
  33.4 4.9 %collective-permute-start = (bf16[32,128]{1,0:T(8,128)(2,1)S(1)}, bf16[32,128]{1,0:T(8,128)(2,1)S(1)}, u32[]{:S(2)}, u32[]{:S(2)}) collective-permute-start(bf16[32,128]{1,0:T(8,128)(2,1)S(1)} %bitcast.26), channel_id=1, source_target_pairs={{0,2},{2,4},{4,6},{6,0},{1,3},{3,5},{5,7},{7,1},{8,10},{10,12},{12... | collective-permute-start | bytes 24584 | tf_op jit(solution)/shard_map/ppermute | solution.py:57
  38.3 1.3 collective-permute-start.3
  49.4 20.3 %copy-start.4 = (bf16[272,512]{1,0:T(8,128)(2,1)}, bf16[272,512]{1,0:T(8,128)(2,1)S(1)}, u32[]{:S(2)}) copy-start(bf16[272,512]{1,0:T(8,128)(2,1)S(1)} %get-tuple-element.42.refs_0_.agg_ref) | copy-start | bytes 835588
  49.4 30.6 %copy-start.25 = (bf16[1,256,512]{2,1,0:T(8,128)(2,1)S(1)}, bf16[1,256,512]{2,1,0:T(8,128)(2,1)}, u32[]{:S(2)}) copy-start(bf16[1,256,512]{2,1,0:T(8,128)(2,1)} %param.21) | copy-start | bytes 786436
  49.4 7.8 %collective-permute-start.5 = (bf16[272,512]{1,0:T(8,128)(2,1)S(1)}, bf16[272,512]{1,0:T(8,128)(2,1)S(1)}, u32[]{:S(2)}, u32[]{:S(2)}) collective-permute-start(bf16[272,512]{1,0:T(8,128)(2,1)S(1)} %get-tuple-element.42.refs_0_.agg_ref), channel_id=1, source_target_pairs={{0,2},{1,7},{2,4},{3,1},{4,6},{5,3},{6,0},{7,5},{8,10},{9,15},{10,... | collective-permute-start | bytes 835592 | tf_op jit(solution)/shard_map/ppermute | solution.py:63
  49.4 7.8 %collective-permute-start.4 = (bf16[272,512]{1,0:T(8,128)(2,1)S(1)}, bf16[272,512]{1,0:T(8,128)(2,1)S(1)}, u32[]{:S(2)}, u32[]{:S(2)}) collective-permute-start(bf16[272,512]{1,0:T(8,128)(2,1)S(1)} %get-tuple-element.42.refs_0_.agg_ref), channel_id=1, source_target_pairs={{0,1},{1,0},{2,3},{3,2},{4,5},{5,4},{6,7},{7,6},{8,9},{9,8},{10,11... | collective-permute-start | bytes 835592 | tf_op jit(solution)/shard_map/ppermute | solution.py:57
  57.2 12.5 %copy-start.18 = (bf16[272,512]{1,0:T(8,128)(2,1)}, bf16[272,512]{1,0:T(8,128)(2,1)S(1)}, u32[]{:S(2)}) copy-start(bf16[272,512]{1,0:T(8,128)(2,1)S(1)} %collective-permute-done.5.refs_2_) | copy-start | bytes 835588
  57.2 7.8 %collective-permute-start.7 = (bf16[272,512]{1,0:T(8,128)(2,1)S(1)}, bf16[272,512]{1,0:T(8,128)(2,1)S(1)}, u32[]{:S(2)}, u32[]{:S(2)}) collective-permute-start(bf16[272,512]{1,0:T(8,128)(2,1)S(1)} %collective-permute-done.5.refs_2_), channel_id=1, source_target_pairs={{0,2},{1,7},{2,4},{3,1},{4,6},{5,3},{6,0},{7,5},{8,10},{9,15},{10,... | collective-permute-start | bytes 835592 | tf_op jit(solution)/shard_map/ppermute | solution.py:63
  57.2 12.5 %copy-start.19 = (bf16[272,512]{1,0:T(8,128)(2,1)}, bf16[272,512]{1,0:T(8,128)(2,1)S(1)}, u32[]{:S(2)}) copy-start(bf16[272,512]{1,0:T(8,128)(2,1)S(1)} %collective-permute-done.4.refs_1_) | copy-start | bytes 835588
  57.2 10.7 %collective-permute-start.6 = (bf16[272,512]{1,0:T(8,128)(2,1)S(1)}, bf16[272,512]{1,0:T(8,128)(2,1)S(1)}, u32[]{:S(2)}, u32[]{:S(2)}) collective-permute-start(bf16[272,512]{1,0:T(8,128)(2,1)S(1)} %collective-permute-done.4.refs_1_), channel_id=1, source_target_pairs={{0,2},{1,7},{2,4},{3,1},{4,6},{5,3},{6,0},{7,5},{8,10},{9,15},{10,... | collective-permute-start | bytes 835592 | tf_op jit(solution)/shard_map/ppermute | solution.py:63
  57.3 10.9 %collective-permute-start.8 = (bf16[272,512]{1,0:T(8,128)(2,1)S(1)}, bf16[272,512]{1,0:T(8,128)(2,1)S(1)}, u32[]{:S(2)}, u32[]{:S(2)}) collective-permute-start(bf16[272,512]{1,0:T(8,128)(2,1)S(1)} %collective-permute-done.5.refs_2_), channel_id=1, source_target_pairs={{0,1},{1,0},{2,3},{3,2},{4,5},{5,4},{6,7},{7,6},{8,9},{9,8},{10,11... | collective-permute-start | bytes 835592 | tf_op jit(solution)/shard_map/ppermute | solution.py:57
  64.9 4.8 %copy-start.20 = (bf16[272,512]{1,0:T(8,128)(2,1)}, bf16[272,512]{1,0:T(8,128)(2,1)S(1)}, u32[]{:S(2)}) copy-start(bf16[272,512]{1,0:T(8,128)(2,1)S(1)} %collective-permute-done.7.refs_4_) | copy-start | bytes 835588
  64.9 3.3 %collective-permute-start.10 = (bf16[272,512]{1,0:T(8,128)(2,1)S(1)}, bf16[272,512]{1,0:T(8,128)(2,1)S(1)}, u32[]{:S(2)}, u32[]{:S(2)}) collective-permute-start(bf16[272,512]{1,0:T(8,128)(2,1)S(1)} %collective-permute-done.7.refs_4_), channel_id=1, source_target_pairs={{0,1},{1,0},{2,3},{3,2},{4,5},{5,4},{6,7},{7,6},{8,9},{9,8},{10,11... | collective-permute-start | bytes 835592 | tf_op jit(solution)/shard_map/ppermute | solution.py:57
  67.9 1.8 collective-permute-start.9
  70.5 25.0 %copy-start.3 = (bf16[4096,1024]{1,0:T(8,128)(2,1)S(1)}, bf16[4096,1024]{1,0:T(8,128)(2,1)}, u32[]{:S(2)}) copy-start(bf16[4096,1024]{1,0:T(8,128)(2,1)} %src) | copy-start | bytes 25165828
  80.0 16.0 %copy-start.7 = (f32[256,1024]{1,0:T(8,128)}, f32[256,1024]{1,0:T(8,128)S(1)}, u32[]{:S(2)}) copy-start(f32[256,1024]{1,0:T(8,128)S(1)} %get-tuple-element.56.dg_ref) | copy-start | bytes 3145732
  80.0 1.5 collective-permute-start.13
  80.1 7.6 %collective-permute-start.11 = (bf16[256,512]{1,0:T(8,128)(2,1)S(1)}, bf16[256,512]{1,0:T(8,128)(2,1)S(1)}, u32[]{:S(2)}, u32[]{:S(2)}) collective-permute-start(bf16[256,512]{1,0:T(8,128)(2,1)S(1)} %bitcast.23), channel_id=1, source_target_pairs={{0,2},{1,7},{2,4},{3,1},{4,6},{5,3},{6,0},{7,5},{8,10},{9,15},{10,... | collective-permute-start | bytes 786440 | tf_op jit(solution)/shard_map/ppermute | solution.py:63
  81.6 14.5 %copy-start.26 = (bf16[256,512]{1,0:T(8,128)(2,1)}, bf16[256,512]{1,0:T(8,128)(2,1)S(1)}, u32[]{:S(2)}) copy-start(bf16[256,512]{1,0:T(8,128)(2,1)S(1)} %collective-permute-done.13.refs_1_) | copy-start | bytes 786436
  81.6 8.9 %collective-permute-start.14 = (bf16[256,512]{1,0:T(8,128)(2,1)S(1)}, bf16[256,512]{1,0:T(8,128)(2,1)S(1)}, u32[]{:S(2)}, u32[]{:S(2)}) collective-permute-start(bf16[256,512]{1,0:T(8,128)(2,1)S(1)} %collective-permute-done.13.refs_1_), channel_id=1, source_target_pairs={{0,2},{1,7},{2,4},{3,1},{4,6},{5,3},{6,0},{7,5},{8,10},{9,15},{10,... | collective-permute-start | bytes 786440 | tf_op jit(solution)/shard_map/ppermute | solution.py:63
  87.7 8.4 %copy-start.27 = (bf16[256,512]{1,0:T(8,128)(2,1)}, bf16[256,512]{1,0:T(8,128)(2,1)S(1)}, u32[]{:S(2)}) copy-start(bf16[256,512]{1,0:T(8,128)(2,1)S(1)} %collective-permute-done.11.refs_2_) | copy-start | bytes 786436
  87.7 7.6 %collective-permute-start.12 = (bf16[256,512]{1,0:T(8,128)(2,1)S(1)}, bf16[256,512]{1,0:T(8,128)(2,1)S(1)}, u32[]{:S(2)}, u32[]{:S(2)}) collective-permute-start(bf16[256,512]{1,0:T(8,128)(2,1)S(1)} %collective-permute-done.11.refs_2_), channel_id=1, source_target_pairs={{0,2},{1,7},{2,4},{3,1},{4,6},{5,3},{6,0},{7,5},{8,10},{9,15},{10,... | collective-permute-start | bytes 786440 | tf_op jit(solution)/shard_map/ppermute | solution.py:63
  87.7 11.7 %collective-permute-start.15 = (bf16[256,512]{1,0:T(8,128)(2,1)S(1)}, bf16[256,512]{1,0:T(8,128)(2,1)S(1)}, u32[]{:S(2)}, u32[]{:S(2)}) collective-permute-start(bf16[256,512]{1,0:T(8,128)(2,1)S(1)} %collective-permute-done.11.refs_2_), channel_id=1, source_target_pairs={{0,1},{1,0},{2,3},{3,2},{4,5},{5,4},{6,7},{7,6},{8,9},{9,8},{10,11... | collective-permute-start | bytes 786440 | tf_op jit(solution)/shard_map/ppermute | solution.py:57
  90.5 5.6 %copy-start.29 = (bf16[256,512]{1,0:T(8,128)(2,1)}, bf16[256,512]{1,0:T(8,128)(2,1)S(1)}, u32[]{:S(2)}) copy-start(bf16[256,512]{1,0:T(8,128)(2,1)S(1)} %collective-permute-done.14.refs_3_) | copy-start | bytes 786436
  90.5 8.9 %collective-permute-start.16 = (bf16[256,512]{1,0:T(8,128)(2,1)S(1)}, bf16[256,512]{1,0:T(8,128)(2,1)S(1)}, u32[]{:S(2)}, u32[]{:S(2)}) collective-permute-start(bf16[256,512]{1,0:T(8,128)(2,1)S(1)} %collective-permute-done.14.refs_3_), channel_id=1, source_target_pairs={{0,1},{1,0},{2,3},{3,2},{4,5},{5,4},{6,7},{7,6},{8,9},{9,8},{10,11... | collective-permute-start | bytes 786440 | tf_op jit(solution)/shard_map/ppermute | solution.py:57
  95.3 4.2 %collective-permute-start.17 = (bf16[256,512]{1,0:T(8,128)(2,1)S(1)}, bf16[256,512]{1,0:T(8,128)(2,1)S(1)}, u32[]{:S(2)}, u32[]{:S(2)}) collective-permute-start(bf16[256,512]{1,0:T(8,128)(2,1)S(1)} %collective-permute-done.12.refs_4_), channel_id=1, source_target_pairs={{0,1},{1,0},{2,3},{3,2},{4,5},{5,4},{6,7},{7,6},{8,9},{9,8},{10,11... | collective-permute-start | bytes 786440 | tf_op jit(solution)/shard_map/ppermute | solution.py:57
  109.8 6.6 %copy-start.2 = (bf16[4096,1024]{1,0:T(8,128)(2,1)S(1)}, bf16[4096,1024]{1,0:T(8,128)(2,1)}, u32[]{:S(2)}) copy-start(bf16[4096,1024]{1,0:T(8,128)(2,1)} %copy-done.1) | copy-start | bytes 25165828
  118.3 2.8 %collective-permute-start.22 = (bf16[4,272,512]{2,1,0:T(8,128)(2,1)S(1)}, bf16[4,272,512]{2,1,0:T(8,128)(2,1)S(1)}, u32[]{:S(2)}, u32[]{:S(2)}) collective-permute-start(bf16[4,272,512]{2,1,0:T(8,128)(2,1)S(1)} %gn_o.1), channel_id=1, source_target_pairs={{0,1},{1,0},{2,3},{3,2},{4,5},{5,4},{6,7},{7,6},{8,9},{9,8},{10,11... | collective-permute-start | bytes 3342344 | tf_op jit(solution)/shard_map/ppermute | solution.py:57
  123.7 22.9 %collective-permute-start.24 = (bf16[272,512]{1,0:T(8,128)(2,1)S(1)}, bf16[272,512]{1,0:T(8,128)(2,1)S(1)}, u32[]{:S(2)}, u32[]{:S(2)}) collective-permute-start(bf16[272,512]{1,0:T(8,128)(2,1)S(1)} %get-tuple-element.63), channel_id=1, source_target_pairs={{0,2},{2,4},{4,6},{6,0},{1,3},{3,5},{5,7},{7,1},{8,10},{10,12},{12... | collective-permute-start | bytes 835592 | tf_op jit(solution)/shard_map/ppermute | solution.py:57
  125.3 24.2 %copy-start.5 = (bf16[272,512]{1,0:T(8,128)(2,1)S(1)}, bf16[272,512]{1,0:T(8,128)(2,1)}, u32[]{:S(2)}) copy-start(bf16[272,512]{1,0:T(8,128)(2,1)} %copy-done.4) | copy-start | bytes 835588
  125.3 24.2 %copy-start.15 = (bf16[1,512]{1,0:T(2,128)(2,1)S(1)}, bf16[1,512]{1,0:T(2,128)(2,1)}, u32[]{:S(2)}) copy-start(bf16[1,512]{1,0:T(2,128)(2,1)} %gain_ref.3) | copy-start | bytes 3076
  125.3 24.2 %copy-start.17 = (bf16[8,256,512]{2,1,0:T(8,128)(2,1)S(1)}, bf16[8,256,512]{2,1,0:T(8,128)(2,1)}, u32[]{:S(2)}) copy-start(bf16[8,256,512]{2,1,0:T(8,128)(2,1)} %copy-done.16) | copy-start | bytes 6291460
  125.3 23.5 %collective-permute-start.25 = (bf16[272,512]{1,0:T(8,128)(2,1)S(1)}, bf16[272,512]{1,0:T(8,128)(2,1)S(1)}, u32[]{:S(2)}, u32[]{:S(2)}) collective-permute-start(bf16[272,512]{1,0:T(8,128)(2,1)S(1)} %get-tuple-element.64), channel_id=1, source_target_pairs={{0,6},{2,0},{4,2},{6,4},{1,7},{3,1},{5,3},{7,5},{8,14},{10,8},{12,... | collective-permute-start | bytes 835592 | tf_op jit(solution)/shard_map/ppermute | solution.py:57
  136.7 9.8 %collective-permute-start.23 = (bf16[272,512]{1,0:T(8,128)(2,1)S(1)}, bf16[272,512]{1,0:T(8,128)(2,1)S(1)}, u32[]{:S(2)}, u32[]{:S(2)}) collective-permute-start(bf16[272,512]{1,0:T(8,128)(2,1)S(1)} %gn_f.1), channel_id=1, source_target_pairs={{0,4},{2,6},{4,0},{6,2},{1,5},{3,7},{5,1},{7,3},{8,12},{10,14},{12... | collective-permute-start | bytes 835592 | tf_op jit(solution)/shard_map/ppermute | solution.py:57
  143.2 36.3 %collective-permute-start.18 = (bf16[4,256,512]{2,1,0:T(8,128)(2,1)}, bf16[4,256,512]{2,1,0:T(8,128)(2,1)S(1)}, u32[]{:S(2)}, u32[]{:S(2)}) collective-permute-start(bf16[4,256,512]{2,1,0:T(8,128)(2,1)} %br_o.1), channel_id=1, source_target_pairs={{0,1},{1,0},{2,3},{3,2},{4,5},{5,4},{6,7},{7,6},{8,9},{9,8},{10,11... | collective-permute-start | bytes 3145736 | tf_op jit(solution)/shard_map/ppermute | solution.py:57
  149.5 24.1 %copy-start.9 = (s32[32]{0:T(128)S(1)}, s32[32]{0:T(128)}, u32[]{:S(2)}) copy-start(s32[32]{0:T(128)} %destination.3) | copy-start | bytes 388
  149.5 24.1 %copy-start.11 = (s32[32]{0:T(128)S(1)}, s32[32]{0:T(128)}, u32[]{:S(2)}) copy-start(s32[32]{0:T(128)} %counts.3) | copy-start | bytes 388
  176.0 15.2 %all-to-all-start.2 = ((bf16[8,96,128]{2,1,0:T(8,128)(2,1)}), bf16[8,96,128]{2,1,0:T(8,128)(2,1)S(1)}, u32[]{:S(2)}, u32[]{:S(2)}) async-start(bf16[8,96,128]{2,1,0:T(8,128)(2,1)} %get-tuple-element.69), calls=%async_computation.2 | async-start | bytes 393216 | tf_op jit(solution)/shard_map/all_to_all | solution.py:520
  181.8 12.9 %collective-permute-start.19 = (bf16[256,512]{1,0:T(8,128)(2,1)S(1)}, bf16[256,512]{1,0:T(8,128)(2,1)S(1)}, u32[]{:S(2)}, u32[]{:S(2)}) collective-permute-start(bf16[256,512]{1,0:T(8,128)(2,1)S(1)} %br_f.1), channel_id=1, source_target_pairs={{0,4},{2,6},{4,0},{6,2},{1,5},{3,7},{5,1},{7,3},{8,12},{10,14},{12... | collective-permute-start | bytes 786440 | tf_op jit(solution)/shard_map/ppermute | solution.py:57
  185.1 10.4 %collective-permute-start.20 = (bf16[256,512]{1,0:T(8,128)(2,1)S(1)}, bf16[256,512]{1,0:T(8,128)(2,1)S(1)}, u32[]{:S(2)}, u32[]{:S(2)}) collective-permute-start(bf16[256,512]{1,0:T(8,128)(2,1)S(1)} %get-tuple-element.52), channel_id=1, source_target_pairs={{0,2},{2,4},{4,6},{6,0},{1,3},{3,5},{5,7},{7,1},{8,10},{10,12},{12... | collective-permute-start | bytes 786440 | tf_op jit(solution)/shard_map/ppermute | solution.py:57
  190.0 6.7 %collective-permute-start.21 = (bf16[256,512]{1,0:T(8,128)(2,1)S(1)}, bf16[256,512]{1,0:T(8,128)(2,1)S(1)}, u32[]{:S(2)}, u32[]{:S(2)}) collective-permute-start(bf16[256,512]{1,0:T(8,128)(2,1)S(1)} %get-tuple-element.53), channel_id=1, source_target_pairs={{0,6},{2,0},{4,2},{6,4},{1,7},{3,1},{5,3},{7,5},{8,14},{10,8},{12,... | collective-permute-start | bytes 786440 | tf_op jit(solution)/shard_map/ppermute | solution.py:57
  191.2 8.2 %collective-permute-start.28 = (bf16[832,128]{1,0:T(8,128)(2,1)S(1)}, bf16[832,128]{1,0:T(8,128)(2,1)S(1)}, u32[]{:S(2)}, u32[]{:S(2)}) collective-permute-start(bf16[832,128]{1,0:T(8,128)(2,1)S(1)} %pad_maximum_fusion.refs_0_), channel_id=1, source_target_pairs={{0,128},{64,192},{128,0},{192,64},{1,129},{65,193},{129,1},{193,65... | collective-permute-start | bytes 638984 | tf_op jit(solution)/shard_map/ppermute | solution.py:57
  192.9 7.3 %collective-permute-start.27 = (bf16[832,128]{1,0:T(8,128)(2,1)S(1)}, bf16[832,128]{1,0:T(8,128)(2,1)S(1)}, u32[]{:S(2)}, u32[]{:S(2)}) collective-permute-start(bf16[832,128]{1,0:T(8,128)(2,1)S(1)} %pad_maximum_fusion.refs_0_), channel_id=1, source_target_pairs={{0,192},{64,0},{128,64},{192,128},{1,193},{65,1},{129,65},{193,129... | collective-permute-start | bytes 638984 | tf_op jit(solution)/shard_map/ppermute | solution.py:57
  194.6 7.1 %collective-permute-start.26 = (bf16[832,128]{1,0:T(8,128)(2,1)S(1)}, bf16[832,128]{1,0:T(8,128)(2,1)S(1)}, u32[]{:S(2)}, u32[]{:S(2)}) collective-permute-start(bf16[832,128]{1,0:T(8,128)(2,1)S(1)} %pad_maximum_fusion.refs_0_), channel_id=1, source_target_pairs={{0,64},{64,128},{128,192},{192,0},{1,65},{65,129},{129,193},{193,1... | collective-permute-start | bytes 638984 | tf_op jit(solution)/shard_map/ppermute | solution.py:57
  (24 other events, 28.4 us)
Sparse Core Ops, SparseCore 0:
  10.6 99.1 all-gather.1
where the time goes:
time: 216 us; the launch traced here: 213 us
  waiting for transfers between devices  67.1 us (31%)
  Pallas kernels  49.9 us (23%)
  starting transfers between devices  45.5 us (21%)
  blocking collectives  18.5 us (9%)
  local copies, waits for them, and re-layouts  16.2 us (8%)
  between operations  14.7 us (7%)
    ppermute x6, waiting for transfers between devices, around(): return lax.ppermute(a, (axis, 'c'), steps)  31.8 us
    ppermute x23, starting transfers between devices, send(): return lax.ppermute(a, axis, [(i, (i + k) % n) for i in range(n)])  30.5 us
    ppermute x23, waiting for transfers between devices, send(): return lax.ppermute(a, axis, [(i, (i + k) % n) for i in range(n)])  19.7 us
    all_to_all x1, blocking collectives, gradient_exchange(): got = lax.all_to_all(outs, ('y', 'z'), 0, 0, tiled=True)  18.5 us
    unnamed x82, local copies, waits for them, and re-layouts  14.8 us
    pallas_call x6, Pallas kernels, nt_call(): pl.pallas_call(functools.partial(nt_kernel, steps, other, kept, sums is n...  14.6 us
    all_to_all x1, starting transfers between devices, local(): mine = lax.all_to_all(ordered, ('y', 'z'), 0, 0, tiled=True)  11.4 us
    pallas_call x1, Pallas kernels, up_call(): pl.pallas_call(up_kernel, grid=(n,), out_shape=(sds((NP, HID), F32), sds(...  8.58 us
  transfers between devices with their start and end apart: 32, of which 22 were waited for; matrix products, arithmetic and copies ran while one was open for 1% of the time, Pallas kernels for 17%

commit v1 on v0

--- a/solution.py
+++ b/solution.py
@@ -273,8 +273,8 @@
     gpf = gp.astype(F32)
     a = gpf * u_ref[0:1, :]
     b = gpf * pre_ref[...]
-    tot[0] += a[:, :128] + a[:, 128:]
-    tot[1] += b[:, :128] + b[:, 128:]
+    for k, p in enumerate((a, b)):
+        tot[k] += sum(p[:, 128 * m:128 * m + 128] for m in range(p.shape[1] // 128))
 
     @pl.when(i == pl.num_programs(0) - 1)
     def _():
@@ -282,7 +282,7 @@
 
 
 def grad_pre(g, down, pre, dg, u):
-    n = 4
+    n = 2
     w = HID // n
 
     def col(r):
@@ -295,7 +295,7 @@
         in_specs=[VM, col(D), col(NP), col(NP), col(8)],
         out_specs=(col(NP), pl.BlockSpec((16, W), lambda i: (0, 0))),
         scratch_shapes=[pltpu.VMEM((2, NP, 128), F32)],
-        compiler_params=params(BIG),
+        compiler_params=params(24),
         cost_estimate=pl.CostEstimate(flops=2 * NP * D * HID, bytes_accessed=12 << 20, transcendentals=0),
         name="grad_pre",
     )(g, hbm(down), hbm(pre), hbm(dg), u)

time: 216 us -> 216 us (level)
  no operation moved by 1% of the time
where the time goes in v1:
time: 216 us; the launch traced here: 213 us
  waiting for transfers between devices  67.1 us (31%)
  Pallas kernels  49.1 us (23%)
  starting transfers between devices  45.8 us (21%)
  blocking collectives  18.5 us (9%)
  local copies, waits for them, and re-layouts  16.8 us (8%)
  between operations  14.7 us (7%)
    ppermute x6, waiting for transfers between devices, around(): return lax.ppermute(a, (axis, 'c'), steps)  31.8 us
    ppermute x23, starting transfers between devices, send(): return lax.ppermute(a, axis, [(i, (i + k) % n) for i in range(n)])  30.8 us
    ppermute x23, waiting for transfers between devices, send(): return lax.ppermute(a, axis, [(i, (i + k) % n) for i in range(n)])  19.7 us
    all_to_all x1, blocking collectives, gradient_exchange(): got = lax.all_to_all(outs, ('y', 'z'), 0, 0, tiled=True)  18.5 us
    unnamed x82, local copies, waits for them, and re-layouts  15.4 us
    pallas_call x6, Pallas kernels, nt_call(): pl.pallas_call(functools.partial(nt_kernel, steps, other, kept, sums is n...  14.6 us
    all_to_all x1, starting transfers between devices, local(): mine = lax.all_to_all(ordered, ('y', 'z'), 0, 0, tiled=True)  11.4 us
    pallas_call x1, Pallas kernels, up_call(): pl.pallas_call(up_kernel, grid=(n,), out_shape=(sds((NP, HID), F32), sds(...  8.58 us
  transfers between devices with their start and end apart: 32, of which 22 were waited for; matrix products, arithmetic and copies ran while one was open for 1% of the time, Pallas kernels for 17%

profile of v1, /device:TPU:32, one launch (start us, length us, event | category | flops | bytes accessed | tf_op | source)
XLA Modules:
  0.0 212.9 jit_solution(3038424733953045086)
XLA Ops:
  9.3 11.4 %all-to-all-start = ((bf16[32,1,128]{2,1,0:T(2,128)(2,1)}), bf16[32,1,128]{2,1,0:T(2,128)(2,1)S(1)}, u32[]{:S(2)}, u32[]{:S(2)}) async-start(bf16[32,1,128]{2,1,0:T(2,128)(2,1)} %copy.18), calls=%async_computation | async-start | bytes 32768 | tf_op jit(solution)/shard_map/all_to_all | solution.py:550
  21.5 7.8 %all-to-all-done = bf16[32,1,128]{2,1,0:T(2,128)(2,1)S(1)} async-done(((bf16[32,1,128]{2,1,0:T(2,128)(2,1)}), bf16[32,1,128]{2,1,0:T(2,128)(2,1)S(1)}, u32[]{:S(2)}, u32[]{:S(2)}) %all-to-all-start) | async-done | bytes 8224 | tf_op jit(solution)/shard_map/all_to_all | solution.py:550
  29.2 3.0 %collective-permute-start.2 = (bf16[32,128]{1,0:T(8,128)(2,1)S(1)}, bf16[32,128]{1,0:T(8,128)(2,1)S(1)}, u32[]{:S(2)}, u32[]{:S(2)}) collective-permute-start(bf16[32,128]{1,0:T(8,128)(2,1)S(1)} %bitcast.24), channel_id=1, source_target_pairs={{0,4},{2,6},{4,0},{6,2},{1,5},{3,7},{5,1},{7,3},{8,12},{10,14},{12... | collective-permute-start | bytes 24584 | tf_op jit(solution)/shard_map/ppermute | solution.py:57
  32.3 1.1 collective-permute-start.1
  33.4 0.9 collective-permute-start
  34.4 1.5 collective-permute-done.1
  35.9 2.4 %collective-permute-done = bf16[32,128]{1,0:T(8,128)(2,1)S(1)} collective-permute-done((bf16[32,128]{1,0:T(8,128)(2,1)S(1)}, bf16[32,128]{1,0:T(8,128)(2,1)S(1)}, u32[]{:S(2)}, u32[]{:S(2)}) %collective-permute-start) | collective-permute-done | bytes 8224 | tf_op jit(solution)/shard_map/ppermute | solution.py:57
  40.9 1.1 copy-done.12
  43.5 4.6 %attn_fwd.1 = (bf16[272,512]{1,0:T(8,128)(2,1)S(1)}, bf16[8,256,512]{2,1,0:T(8,128)(2,1)S(1)}, f32[256,128]{1,0:T(8,128)S(1)}, bf16[256,128]{1,0:T(8,128)(2,1)S(1)}) custom-call(s32[4]{0:T(128)S(1)} %pad_add_fusion.info, s32[32]{0:T(128)S(1)} %copy-done.8, s32[32]{0:T(128)S(1)} %copy-done.10, s32[256]{0:T(256)S(1)} %reshape.24.var_ids.ids, ...), custom_call_target="tpu_custom_call" | custom-call | flops 805306368 | bytes 4194304 | tf_op jit(solution)/shard_map/attn_fwd/pallas_call | solution.py:150
  48.1 1.3 copy-done.16
  49.6 7.6 %collective-permute-done.5.refs_2_ = bf16[272,512]{1,0:T(8,128)(2,1)S(1)} collective-permute-done((bf16[272,512]{1,0:T(8,128)(2,1)S(1)}, bf16[272,512]{1,0:T(8,128)(2,1)S(1)}, u32[]{:S(2)}, u32[]{:S(2)}) %collective-permute-start.5) | collective-permute-done | bytes 278560 | tf_op jit(solution)/shard_map/ppermute | solution.py:63
  57.4 7.5 %collective-permute-done.7.refs_4_ = bf16[272,512]{1,0:T(8,128)(2,1)S(1)} collective-permute-done((bf16[272,512]{1,0:T(8,128)(2,1)S(1)}, bf16[272,512]{1,0:T(8,128)(2,1)S(1)}, u32[]{:S(2)}, u32[]{:S(2)}) %collective-permute-start.7) | collective-permute-done | bytes 278560 | tf_op jit(solution)/shard_map/ppermute | solution.py:63
  64.9 3.0 %collective-permute-done.6.refs_3_ = bf16[272,512]{1,0:T(8,128)(2,1)S(1)} collective-permute-done((bf16[272,512]{1,0:T(8,128)(2,1)S(1)}, bf16[272,512]{1,0:T(8,128)(2,1)S(1)}, u32[]{:S(2)}, u32[]{:S(2)}) %collective-permute-start.6) | collective-permute-done | bytes 278560 | tf_op jit(solution)/shard_map/ppermute | solution.py:63
  68.2 1.5 collective-permute-done.9.refs_6_
  70.5 8.6 %ln_up.1 = (f32[256,1024]{1,0:T(8,128)S(1)}, f32[256,1024]{1,0:T(8,128)S(1)}, bf16[256,1024]{1,0:T(8,128)(2,1)S(1)}, f32[8,1024]{1,0:T(8,128)S(1)}, f32[2,256,128]{2,1,0:T(8,128)S(1)}) custom-call(s32[4]{0:T(128)S(1)} %pad_add_fusion.info, bf16[272,512]{1,0:T(8,128)(2,1)} %copy-done.4, bf16[272,512]{1,0:T(8,128)(2,1)} %copy-done.19, ...), custom_call_target="tpu_custom_call" | custom-call | flops 2281701376 | bytes 16777216 | tf_op jit(solution)/shard_map/ln_up/pallas_call | solution.py:219
  79.1 1.0 copy-done.6
  80.1 1.4 collective-permute-done.13.refs_1_
  81.6 6.1 %collective-permute-done.11.refs_2_ = bf16[256,512]{1,0:T(8,128)(2,1)S(1)} collective-permute-done((bf16[256,512]{1,0:T(8,128)(2,1)S(1)}, bf16[256,512]{1,0:T(8,128)(2,1)S(1)}, u32[]{:S(2)}, u32[]{:S(2)}) %collective-permute-start.11) | collective-permute-done | bytes 262176 | tf_op jit(solution)/shard_map/ppermute | solution.py:63
  87.7 2.8 %collective-permute-done.14.refs_3_ = bf16[256,512]{1,0:T(8,128)(2,1)S(1)} collective-permute-done((bf16[256,512]{1,0:T(8,128)(2,1)S(1)}, bf16[256,512]{1,0:T(8,128)(2,1)S(1)}, u32[]{:S(2)}, u32[]{:S(2)}) %collective-permute-start.14) | collective-permute-done | bytes 262176 | tf_op jit(solution)/shard_map/ppermute | solution.py:63
  90.5 4.8 %collective-permute-done.12.refs_4_ = bf16[256,512]{1,0:T(8,128)(2,1)S(1)} collective-permute-done((bf16[256,512]{1,0:T(8,128)(2,1)S(1)}, bf16[256,512]{1,0:T(8,128)(2,1)S(1)}, u32[]{:S(2)}, u32[]{:S(2)}) %collective-permute-start.12) | collective-permute-done | bytes 262176 | tf_op jit(solution)/shard_map/ppermute | solution.py:63
  96.1 3.3 %copy-done.1 = bf16[4096,1024]{1,0:T(8,128)(2,1)} copy-done((bf16[4096,1024]{1,0:T(8,128)(2,1)}, bf16[4096,1024]{1,0:T(8,128)(2,1)S(1)}, u32[]{:S(2)}) %copy-start.1) | copy-done | bytes 8388632
  100.9 1.7 join.1.g
  102.6 7.2 %all-gather.2.cloned.1.call-done.rhs_ref.down_ref = bf16[4096,1024]{1,0:T(8,128)(2,1)} async-done(((bf16[128,1024]{1,0:T(8,128)(2,1)}), bf16[4096,1024]{1,0:T(8,128)(2,1)}) %all-gather.2.cloned.1.call-update) | async-done | bytes 8388624 | tf_op jit(solution)/shard_map/all_gather | solution.py:546
  109.8 5.7 %grad_pre.1 = (bf16[256,1024]{1,0:T(8,128)(2,1)S(1)}, bf16[16,512]{1,0:T(8,128)(2,1)S(1)}) custom-call(bf16[256,4096]{1,0:T(8,128)(2,1)S(1)} %join.1.g, bf16[4096,1024]{1,0:T(8,128)(2,1)} %all-gather.2.cloned.1.call-done.rhs_ref.down_ref, f32[256,1024]{1,0:T(8,128)} %copy-done.6, f32[256,1024]{1,0:T(8,128)} %copy-done.7, f32[8,1024]{1,0:T(8,128)S(1)} %get-tuple-element.44.u_ref), custom_call_target="tpu_custom_call" | custom-call | flops 2147483648 | bytes 12582912 | tf_op jit(solution)/shard_map/grad_pre/pallas_call | solution.py:291
  116.3 1.8 gn_o.1
  118.2 2.7 %collective-permute-done.22.refs_1_ = bf16[4,272,512]{2,1,0:T(8,128)(2,1)S(1)} collective-permute-done((bf16[4,272,512]{2,1,0:T(8,128)(2,1)S(1)}, bf16[4,272,512]{2,1,0:T(8,128)(2,1)S(1)}, u32[]{:S(2)}, u32[]{:S(2)}) %collective-permute-start.22) | collective-permute-done | bytes 1114144 | tf_op jit(solution)/shard_map/ppermute | solution.py:57
  121.0 1.0 gn_f.1
  122.0 1.6 gn_n.1
  123.6 1.5 collective-permute-start.24
  125.1 11.7 %collective-permute-start.25 = (bf16[272,512]{1,0:T(8,128)(2,1)S(1)}, bf16[272,512]{1,0:T(8,128)(2,1)S(1)}, u32[]{:S(2)}, u32[]{:S(2)}) collective-permute-start(bf16[272,512]{1,0:T(8,128)(2,1)S(1)} %get-tuple-element.64), channel_id=1, source_target_pairs={{0,6},{2,0},{4,2},{6,4},{1,7},{3,1},{5,3},{7,5},{8,14},{10,8},{12,... | collective-permute-start | bytes 835592 | tf_op jit(solution)/shard_map/ppermute | solution.py:57
  136.8 1.8 collective-permute-start.23
  138.6 4.7 %br_o.1 = bf16[4,256,512]{2,1,0:T(8,128)(2,1)} custom-call(s32[4]{0:T(128)S(1)} %pad_add_fusion.info, bf16[256,1024]{1,0:T(8,128)(2,1)S(1)} %get-tuple-element.49.lhs_ref, bf16[4096,1024]{1,0:T(8,128)(2,1)} %all-gather.2.cloned.1.call-done.rhs_ref.down_ref), custom_call_target="tpu_custom_call" | custom-call | flops 1073741824 | bytes 4194304 | tf_op jit(solution)/shard_map/br_o/pallas_call | solution.py:367
  143.3 3.2 %collective-permute-done.23.b_ref = bf16[272,512]{1,0:T(8,128)(2,1)S(1)} collective-permute-done((bf16[272,512]{1,0:T(8,128)(2,1)S(1)}, bf16[272,512]{1,0:T(8,128)(2,1)S(1)}, u32[]{:S(2)}, u32[]{:S(2)}) %collective-permute-start.23) | collective-permute-done | bytes 278560 | tf_op jit(solution)/shard_map/ppermute | solution.py:57
  146.7 2.2 %collective-permute-done.25.p2_ref = bf16[272,512]{1,0:T(8,128)(2,1)S(1)} collective-permute-done((bf16[272,512]{1,0:T(8,128)(2,1)S(1)}, bf16[272,512]{1,0:T(8,128)(2,1)S(1)}, u32[]{:S(2)}, u32[]{:S(2)}) %collective-permute-start.25) | collective-permute-done | bytes 278560 | tf_op jit(solution)/shard_map/ppermute | solution.py:57
  149.6 5.6 %attn_bwd.1 = bf16[32,32,128]{2,1,0:T(8,128)(2,1)S(1)} custom-call(f32[272,512]{1,0:T(8,128)S(1)} %gn_p.1.own_ref, bf16[272,512]{1,0:T(8,128)(2,1)} %copy-done.38, bf16[272,512]{1,0:T(8,128)(2,1)} %copy-done.39, bf16[272,512]{1,0:T(8,128)(2,1)S(1)} %copy-done.5, f32[2,256,128]{2,1,0:T(8,128)S(1)} %get-tuple-element.65.st_ref, bf16[1,512]{1,0:T(2,128)(2,1)S(1)} %copy-done.15, ...), custom_call_target="tpu_custom_call" | custom-call | flops 1610612736 | bytes 5242880 | tf_op jit(solution)/shard_map/attn_bwd/pallas_call | solution.py:470
  155.2 18.5 %all_to_all.22.got_ref = bf16[32,32,128]{2,1,0:T(8,128)(2,1)S(1)} all-to-all(bf16[32,32,128]{2,1,0:T(8,128)(2,1)S(1)} %attn_bwd.1), channel_id=1, replica_groups=mesh['y'=4,'z'=8,'x'=4,'c'=2] {'y','z'}, dimensions={0} | all-to-all | bytes 524288 | tf_op jit(solution)/shard_map/all_to_all | solution.py:513
  173.7 2.4 %slot_sum.1 = (bf16[8,96,128]{2,1,0:T(8,128)(2,1)}, bf16[64,128]{1,0:T(8,128)(2,1)S(1)}) custom-call(s32[32]{0:T(128)S(1)} %copy-done.9, s32[32]{0:T(128)S(1)} %copy-done.11, s32[256]{0:T(256)S(1)} %reshape.24.var_ids.ids, bf16[32,32,128]{2,1,0:T(8,128)(2,1)S(1)} %all_to_all.22.got_ref), custom_call_target="tpu_custom_call" | custom-call | flops 1048576 | bytes 2097152 | tf_op jit(solution)/shard_map/slot_sum/pallas_call | solution.py:514
  176.1 3.5 %all-to-all-start.2 = ((bf16[8,96,128]{2,1,0:T(8,128)(2,1)}), bf16[8,96,128]{2,1,0:T(8,128)(2,1)S(1)}, u32[]{:S(2)}, u32[]{:S(2)}) async-start(bf16[8,96,128]{2,1,0:T(8,128)(2,1)} %get-tuple-element.69), calls=%async_computation.2 | async-start | bytes 393216 | tf_op jit(solution)/shard_map/all_to_all | solution.py:520
  179.6 2.3 %br_f.1 = bf16[256,512]{1,0:T(8,128)(2,1)S(1)} custom-call(s32[4]{0:T(128)S(1)} %pad_add_fusion.info, bf16[256,1024]{1,0:T(8,128)(2,1)S(1)} %get-tuple-element.49.lhs_ref, bf16[4096,1024]{1,0:T(8,128)(2,1)} %all-gather.2.cloned.1.call-done.rhs_ref.down_ref, bf16[4,256,512]{2,1,0:T(8,128)(2,1)S(1)} %collective-permute-done.18.refs_0_), custom_call_target="tpu_custom_call" | custom-call | flops 268435456 | bytes 1048576 | tf_op jit(solution)/shard_map/br_f/pallas_call | solution.py:367
  181.9 3.2 %br_n.1 = (bf16[256,512]{1,0:T(8,128)(2,1)S(1)}, bf16[256,512]{1,0:T(8,128)(2,1)S(1)}, bf16[256,512]{1,0:T(8,128)(2,1)S(1)}) custom-call(s32[4]{0:T(128)S(1)} %pad_add_fusion.info, bf16[256,1024]{1,0:T(8,128)(2,1)S(1)} %get-tuple-element.49.lhs_ref, bf16[4096,1024]{1,0:T(8,128)(2,1)} %all-gather.2.cloned.1.call-done.rhs_ref.down_ref, ...), custom_call_target="tpu_custom_call" | custom-call | flops 805306368 | bytes 3145728 | tf_op jit(solution)/shard_map/br_n/pallas_call | solution.py:367
  185.2 5.0 %collective-permute-start.20 = (bf16[256,512]{1,0:T(8,128)(2,1)S(1)}, bf16[256,512]{1,0:T(8,128)(2,1)S(1)}, u32[]{:S(2)}, u32[]{:S(2)}) collective-permute-start(bf16[256,512]{1,0:T(8,128)(2,1)S(1)} %get-tuple-element.52), channel_id=1, source_target_pairs={{0,2},{2,4},{4,6},{6,0},{1,3},{3,5},{5,7},{7,1},{8,10},{10,12},{12... | collective-permute-start | bytes 786440 | tf_op jit(solution)/shard_map/ppermute | solution.py:57
  190.2 1.2 collective-permute-start.21
  191.4 1.6 collective-permute-start.28
  193.0 1.8 collective-permute-start.27
  195.7 1.2 collective-permute-done.21.p2
  197.5 1.8 mix.1
  200.4 1.5 collective-permute-done.26.refs_1_
  202.6 3.3 %spread.1 = (f32[48,16,512]{2,1,0:T(8,128)}, f32[48,512]{1,0:T(8,128)}, f32[1,512]{1,0:T(1,128)}) custom-call(s32[4]{0:T(128)S(1)} %pad_add_fusion.info, bf16[832,128]{1,0:T(8,128)(2,1)S(1)} %pad_maximum_fusion.refs_0_, bf16[832,128]{1,0:T(8,128)(2,1)} %copy-done.37, bf16[832,128]{1,0:T(8,128)(2,1)} %copy-done.36, bf16[832,128]{1,0:T(8,128)(2,1)} %copy-done.35), custom_call_target="tpu_custom_call" | custom-call | flops 1048576 | bytes 3145728 | tf_op jit(solution)/shard_map/spread/pallas_call | solution.py:523
  (125 shorter events, 15.9 us)
Async XLA Ops:
  7.2 102.7 %all-gather.2.cloned.1.call-start = ((), (), s32[]{:S(2)}) async-start(), calls=%async_computation.3 | async-start | bytes 8650752 | tf_op jit(solution)/shard_map/all_gather | solution.py:546
  9.3 19.9 %all-to-all-start = ((bf16[32,1,128]{2,1,0:T(2,128)(2,1)}), bf16[32,1,128]{2,1,0:T(2,128)(2,1)S(1)}, u32[]{:S(2)}, u32[]{:S(2)}) async-start(bf16[32,1,128]{2,1,0:T(2,128)(2,1)} %copy.18), calls=%async_computation | async-start | bytes 32768 | tf_op jit(solution)/shard_map/all_to_all | solution.py:550
  29.2 5.2 %collective-permute-start.2 = (bf16[32,128]{1,0:T(8,128)(2,1)S(1)}, bf16[32,128]{1,0:T(8,128)(2,1)S(1)}, u32[]{:S(2)}, u32[]{:S(2)}) collective-permute-start(bf16[32,128]{1,0:T(8,128)(2,1)S(1)} %bitcast.24), channel_id=1, source_target_pairs={{0,4},{2,6},{4,0},{6,2},{1,5},{3,7},{5,1},{7,3},{8,12},{10,14},{12... | collective-permute-start | bytes 24584 | tf_op jit(solution)/shard_map/ppermute | solution.py:57
  32.3 3.7 %collective-permute-start.1 = (bf16[32,128]{1,0:T(8,128)(2,1)S(1)}, bf16[32,128]{1,0:T(8,128)(2,1)S(1)}, u32[]{:S(2)}, u32[]{:S(2)}) collective-permute-start(bf16[32,128]{1,0:T(8,128)(2,1)S(1)} %bitcast.25), channel_id=1, source_target_pairs={{0,6},{2,0},{4,2},{6,4},{1,7},{3,1},{5,3},{7,5},{8,14},{10,8},{12,... | collective-permute-start | bytes 24584 | tf_op jit(solution)/shard_map/ppermute | solution.py:57
  33.4 4.9 %collective-permute-start = (bf16[32,128]{1,0:T(8,128)(2,1)S(1)}, bf16[32,128]{1,0:T(8,128)(2,1)S(1)}, u32[]{:S(2)}, u32[]{:S(2)}) collective-permute-start(bf16[32,128]{1,0:T(8,128)(2,1)S(1)} %bitcast.26), channel_id=1, source_target_pairs={{0,2},{2,4},{4,6},{6,0},{1,3},{3,5},{5,7},{7,1},{8,10},{10,12},{12... | collective-permute-start | bytes 24584 | tf_op jit(solution)/shard_map/ppermute | solution.py:57
  38.3 1.3 collective-permute-start.3
  49.4 20.3 %copy-start.4 = (bf16[272,512]{1,0:T(8,128)(2,1)}, bf16[272,512]{1,0:T(8,128)(2,1)S(1)}, u32[]{:S(2)}) copy-start(bf16[272,512]{1,0:T(8,128)(2,1)S(1)} %get-tuple-element.42.refs_0_.agg_ref) | copy-start | bytes 835588
  49.4 30.6 %copy-start.25 = (bf16[1,256,512]{2,1,0:T(8,128)(2,1)S(1)}, bf16[1,256,512]{2,1,0:T(8,128)(2,1)}, u32[]{:S(2)}) copy-start(bf16[1,256,512]{2,1,0:T(8,128)(2,1)} %param.21) | copy-start | bytes 786436
  49.4 7.8 %collective-permute-start.5 = (bf16[272,512]{1,0:T(8,128)(2,1)S(1)}, bf16[272,512]{1,0:T(8,128)(2,1)S(1)}, u32[]{:S(2)}, u32[]{:S(2)}) collective-permute-start(bf16[272,512]{1,0:T(8,128)(2,1)S(1)} %get-tuple-element.42.refs_0_.agg_ref), channel_id=1, source_target_pairs={{0,2},{1,7},{2,4},{3,1},{4,6},{5,3},{6,0},{7,5},{8,10},{9,15},{10,... | collective-permute-start | bytes 835592 | tf_op jit(solution)/shard_map/ppermute | solution.py:63
  49.4 7.8 %collective-permute-start.4 = (bf16[272,512]{1,0:T(8,128)(2,1)S(1)}, bf16[272,512]{1,0:T(8,128)(2,1)S(1)}, u32[]{:S(2)}, u32[]{:S(2)}) collective-permute-start(bf16[272,512]{1,0:T(8,128)(2,1)S(1)} %get-tuple-element.42.refs_0_.agg_ref), channel_id=1, source_target_pairs={{0,1},{1,0},{2,3},{3,2},{4,5},{5,4},{6,7},{7,6},{8,9},{9,8},{10,11... | collective-permute-start | bytes 835592 | tf_op jit(solution)/shard_map/ppermute | solution.py:57
  57.2 12.5 %copy-start.18 = (bf16[272,512]{1,0:T(8,128)(2,1)}, bf16[272,512]{1,0:T(8,128)(2,1)S(1)}, u32[]{:S(2)}) copy-start(bf16[272,512]{1,0:T(8,128)(2,1)S(1)} %collective-permute-done.5.refs_2_) | copy-start | bytes 835588
  57.2 7.8 %collective-permute-start.7 = (bf16[272,512]{1,0:T(8,128)(2,1)S(1)}, bf16[272,512]{1,0:T(8,128)(2,1)S(1)}, u32[]{:S(2)}, u32[]{:S(2)}) collective-permute-start(bf16[272,512]{1,0:T(8,128)(2,1)S(1)} %collective-permute-done.5.refs_2_), channel_id=1, source_target_pairs={{0,2},{1,7},{2,4},{3,1},{4,6},{5,3},{6,0},{7,5},{8,10},{9,15},{10,... | collective-permute-start | bytes 835592 | tf_op jit(solution)/shard_map/ppermute | solution.py:63
  57.2 12.5 %copy-start.19 = (bf16[272,512]{1,0:T(8,128)(2,1)}, bf16[272,512]{1,0:T(8,128)(2,1)S(1)}, u32[]{:S(2)}) copy-start(bf16[272,512]{1,0:T(8,128)(2,1)S(1)} %collective-permute-done.4.refs_1_) | copy-start | bytes 835588
  57.2 10.7 %collective-permute-start.6 = (bf16[272,512]{1,0:T(8,128)(2,1)S(1)}, bf16[272,512]{1,0:T(8,128)(2,1)S(1)}, u32[]{:S(2)}, u32[]{:S(2)}) collective-permute-start(bf16[272,512]{1,0:T(8,128)(2,1)S(1)} %collective-permute-done.4.refs_1_), channel_id=1, source_target_pairs={{0,2},{1,7},{2,4},{3,1},{4,6},{5,3},{6,0},{7,5},{8,10},{9,15},{10,... | collective-permute-start | bytes 835592 | tf_op jit(solution)/shard_map/ppermute | solution.py:63
  57.3 10.9 %collective-permute-start.8 = (bf16[272,512]{1,0:T(8,128)(2,1)S(1)}, bf16[272,512]{1,0:T(8,128)(2,1)S(1)}, u32[]{:S(2)}, u32[]{:S(2)}) collective-permute-start(bf16[272,512]{1,0:T(8,128)(2,1)S(1)} %collective-permute-done.5.refs_2_), channel_id=1, source_target_pairs={{0,1},{1,0},{2,3},{3,2},{4,5},{5,4},{6,7},{7,6},{8,9},{9,8},{10,11... | collective-permute-start | bytes 835592 | tf_op jit(solution)/shard_map/ppermute | solution.py:57
  64.9 4.8 %copy-start.20 = (bf16[272,512]{1,0:T(8,128)(2,1)}, bf16[272,512]{1,0:T(8,128)(2,1)S(1)}, u32[]{:S(2)}) copy-start(bf16[272,512]{1,0:T(8,128)(2,1)S(1)} %collective-permute-done.7.refs_4_) | copy-start | bytes 835588
  64.9 3.3 %collective-permute-start.10 = (bf16[272,512]{1,0:T(8,128)(2,1)S(1)}, bf16[272,512]{1,0:T(8,128)(2,1)S(1)}, u32[]{:S(2)}, u32[]{:S(2)}) collective-permute-start(bf16[272,512]{1,0:T(8,128)(2,1)S(1)} %collective-permute-done.7.refs_4_), channel_id=1, source_target_pairs={{0,1},{1,0},{2,3},{3,2},{4,5},{5,4},{6,7},{7,6},{8,9},{9,8},{10,11... | collective-permute-start | bytes 835592 | tf_op jit(solution)/shard_map/ppermute | solution.py:57
  67.9 1.8 collective-permute-start.9
  70.5 25.0 %copy-start.3 = (bf16[4096,1024]{1,0:T(8,128)(2,1)S(1)}, bf16[4096,1024]{1,0:T(8,128)(2,1)}, u32[]{:S(2)}) copy-start(bf16[4096,1024]{1,0:T(8,128)(2,1)} %src) | copy-start | bytes 25165828
  80.0 16.0 %copy-start.7 = (f32[256,1024]{1,0:T(8,128)}, f32[256,1024]{1,0:T(8,128)S(1)}, u32[]{:S(2)}) copy-start(f32[256,1024]{1,0:T(8,128)S(1)} %get-tuple-element.56.dg_ref) | copy-start | bytes 3145732
  80.0 1.5 collective-permute-start.13
  80.1 7.6 %collective-permute-start.11 = (bf16[256,512]{1,0:T(8,128)(2,1)S(1)}, bf16[256,512]{1,0:T(8,128)(2,1)S(1)}, u32[]{:S(2)}, u32[]{:S(2)}) collective-permute-start(bf16[256,512]{1,0:T(8,128)(2,1)S(1)} %bitcast.23), channel_id=1, source_target_pairs={{0,2},{1,7},{2,4},{3,1},{4,6},{5,3},{6,0},{7,5},{8,10},{9,15},{10,... | collective-permute-start | bytes 786440 | tf_op jit(solution)/shard_map/ppermute | solution.py:63
  81.6 14.5 %copy-start.26 = (bf16[256,512]{1,0:T(8,128)(2,1)}, bf16[256,512]{1,0:T(8,128)(2,1)S(1)}, u32[]{:S(2)}) copy-start(bf16[256,512]{1,0:T(8,128)(2,1)S(1)} %collective-permute-done.13.refs_1_) | copy-start | bytes 786436
  81.6 8.9 %collective-permute-start.14 = (bf16[256,512]{1,0:T(8,128)(2,1)S(1)}, bf16[256,512]{1,0:T(8,128)(2,1)S(1)}, u32[]{:S(2)}, u32[]{:S(2)}) collective-permute-start(bf16[256,512]{1,0:T(8,128)(2,1)S(1)} %collective-permute-done.13.refs_1_), channel_id=1, source_target_pairs={{0,2},{1,7},{2,4},{3,1},{4,6},{5,3},{6,0},{7,5},{8,10},{9,15},{10,... | collective-permute-start | bytes 786440 | tf_op jit(solution)/shard_map/ppermute | solution.py:63
  87.7 8.4 %copy-start.27 = (bf16[256,512]{1,0:T(8,128)(2,1)}, bf16[256,512]{1,0:T(8,128)(2,1)S(1)}, u32[]{:S(2)}) copy-start(bf16[256,512]{1,0:T(8,128)(2,1)S(1)} %collective-permute-done.11.refs_2_) | copy-start | bytes 786436
  87.7 7.6 %collective-permute-start.12 = (bf16[256,512]{1,0:T(8,128)(2,1)S(1)}, bf16[256,512]{1,0:T(8,128)(2,1)S(1)}, u32[]{:S(2)}, u32[]{:S(2)}) collective-permute-start(bf16[256,512]{1,0:T(8,128)(2,1)S(1)} %collective-permute-done.11.refs_2_), channel_id=1, source_target_pairs={{0,2},{1,7},{2,4},{3,1},{4,6},{5,3},{6,0},{7,5},{8,10},{9,15},{10,... | collective-permute-start | bytes 786440 | tf_op jit(solution)/shard_map/ppermute | solution.py:63
  87.7 11.7 %collective-permute-start.15 = (bf16[256,512]{1,0:T(8,128)(2,1)S(1)}, bf16[256,512]{1,0:T(8,128)(2,1)S(1)}, u32[]{:S(2)}, u32[]{:S(2)}) collective-permute-start(bf16[256,512]{1,0:T(8,128)(2,1)S(1)} %collective-permute-done.11.refs_2_), channel_id=1, source_target_pairs={{0,1},{1,0},{2,3},{3,2},{4,5},{5,4},{6,7},{7,6},{8,9},{9,8},{10,11... | collective-permute-start | bytes 786440 | tf_op jit(solution)/shard_map/ppermute | solution.py:57
  90.5 5.6 %copy-start.29 = (bf16[256,512]{1,0:T(8,128)(2,1)}, bf16[256,512]{1,0:T(8,128)(2,1)S(1)}, u32[]{:S(2)}) copy-start(bf16[256,512]{1,0:T(8,128)(2,1)S(1)} %collective-permute-done.14.refs_3_) | copy-start | bytes 786436
  90.5 8.9 %collective-permute-start.16 = (bf16[256,512]{1,0:T(8,128)(2,1)S(1)}, bf16[256,512]{1,0:T(8,128)(2,1)S(1)}, u32[]{:S(2)}, u32[]{:S(2)}) collective-permute-start(bf16[256,512]{1,0:T(8,128)(2,1)S(1)} %collective-permute-done.14.refs_3_), channel_id=1, source_target_pairs={{0,1},{1,0},{2,3},{3,2},{4,5},{5,4},{6,7},{7,6},{8,9},{9,8},{10,11... | collective-permute-start | bytes 786440 | tf_op jit(solution)/shard_map/ppermute | solution.py:57
  95.3 4.2 %collective-permute-start.17 = (bf16[256,512]{1,0:T(8,128)(2,1)S(1)}, bf16[256,512]{1,0:T(8,128)(2,1)S(1)}, u32[]{:S(2)}, u32[]{:S(2)}) collective-permute-start(bf16[256,512]{1,0:T(8,128)(2,1)S(1)} %collective-permute-done.12.refs_4_), channel_id=1, source_target_pairs={{0,1},{1,0},{2,3},{3,2},{4,5},{5,4},{6,7},{7,6},{8,9},{9,8},{10,11... | collective-permute-start | bytes 786440 | tf_op jit(solution)/shard_map/ppermute | solution.py:57
  109.8 6.5 %copy-start.2 = (bf16[4096,1024]{1,0:T(8,128)(2,1)S(1)}, bf16[4096,1024]{1,0:T(8,128)(2,1)}, u32[]{:S(2)}) copy-start(bf16[4096,1024]{1,0:T(8,128)(2,1)} %copy-done.1) | copy-start | bytes 25165828
  118.1 2.8 %collective-permute-start.22 = (bf16[4,272,512]{2,1,0:T(8,128)(2,1)S(1)}, bf16[4,272,512]{2,1,0:T(8,128)(2,1)S(1)}, u32[]{:S(2)}, u32[]{:S(2)}) collective-permute-start(bf16[4,272,512]{2,1,0:T(8,128)(2,1)S(1)} %gn_o.1), channel_id=1, source_target_pairs={{0,1},{1,0},{2,3},{3,2},{4,5},{5,4},{6,7},{7,6},{8,9},{9,8},{10,11... | collective-permute-start | bytes 3342344 | tf_op jit(solution)/shard_map/ppermute | solution.py:57
  123.6 23.1 %collective-permute-start.24 = (bf16[272,512]{1,0:T(8,128)(2,1)S(1)}, bf16[272,512]{1,0:T(8,128)(2,1)S(1)}, u32[]{:S(2)}, u32[]{:S(2)}) collective-permute-start(bf16[272,512]{1,0:T(8,128)(2,1)S(1)} %get-tuple-element.63), channel_id=1, source_target_pairs={{0,2},{2,4},{4,6},{6,0},{1,3},{3,5},{5,7},{7,1},{8,10},{10,12},{12... | collective-permute-start | bytes 835592 | tf_op jit(solution)/shard_map/ppermute | solution.py:57
  125.1 24.5 %copy-start.5 = (bf16[272,512]{1,0:T(8,128)(2,1)S(1)}, bf16[272,512]{1,0:T(8,128)(2,1)}, u32[]{:S(2)}) copy-start(bf16[272,512]{1,0:T(8,128)(2,1)} %copy-done.4) | copy-start | bytes 835588
  125.1 24.5 %copy-start.15 = (bf16[1,512]{1,0:T(2,128)(2,1)S(1)}, bf16[1,512]{1,0:T(2,128)(2,1)}, u32[]{:S(2)}) copy-start(bf16[1,512]{1,0:T(2,128)(2,1)} %gain_ref.3) | copy-start | bytes 3076
  125.1 24.5 %copy-start.17 = (bf16[8,256,512]{2,1,0:T(8,128)(2,1)S(1)}, bf16[8,256,512]{2,1,0:T(8,128)(2,1)}, u32[]{:S(2)}) copy-start(bf16[8,256,512]{2,1,0:T(8,128)(2,1)} %copy-done.16) | copy-start | bytes 6291460
  125.1 23.8 %collective-permute-start.25 = (bf16[272,512]{1,0:T(8,128)(2,1)S(1)}, bf16[272,512]{1,0:T(8,128)(2,1)S(1)}, u32[]{:S(2)}, u32[]{:S(2)}) collective-permute-start(bf16[272,512]{1,0:T(8,128)(2,1)S(1)} %get-tuple-element.64), channel_id=1, source_target_pairs={{0,6},{2,0},{4,2},{6,4},{1,7},{3,1},{5,3},{7,5},{8,14},{10,8},{12,... | collective-permute-start | bytes 835592 | tf_op jit(solution)/shard_map/ppermute | solution.py:57
  136.8 9.8 %collective-permute-start.23 = (bf16[272,512]{1,0:T(8,128)(2,1)S(1)}, bf16[272,512]{1,0:T(8,128)(2,1)S(1)}, u32[]{:S(2)}, u32[]{:S(2)}) collective-permute-start(bf16[272,512]{1,0:T(8,128)(2,1)S(1)} %gn_f.1), channel_id=1, source_target_pairs={{0,4},{2,6},{4,0},{6,2},{1,5},{3,7},{5,1},{7,3},{8,12},{10,14},{12... | collective-permute-start | bytes 835592 | tf_op jit(solution)/shard_map/ppermute | solution.py:57
  143.2 36.3 %collective-permute-start.18 = (bf16[4,256,512]{2,1,0:T(8,128)(2,1)}, bf16[4,256,512]{2,1,0:T(8,128)(2,1)S(1)}, u32[]{:S(2)}, u32[]{:S(2)}) collective-permute-start(bf16[4,256,512]{2,1,0:T(8,128)(2,1)} %br_o.1), channel_id=1, source_target_pairs={{0,1},{1,0},{2,3},{3,2},{4,5},{5,4},{6,7},{7,6},{8,9},{9,8},{10,11... | collective-permute-start | bytes 3145736 | tf_op jit(solution)/shard_map/ppermute | solution.py:57
  149.6 24.1 %copy-start.9 = (s32[32]{0:T(128)S(1)}, s32[32]{0:T(128)}, u32[]{:S(2)}) copy-start(s32[32]{0:T(128)} %destination.3) | copy-start | bytes 388
  149.6 24.1 %copy-start.11 = (s32[32]{0:T(128)S(1)}, s32[32]{0:T(128)}, u32[]{:S(2)}) copy-start(s32[32]{0:T(128)} %counts.3) | copy-start | bytes 388
  176.1 15.3 %all-to-all-start.2 = ((bf16[8,96,128]{2,1,0:T(8,128)(2,1)}), bf16[8,96,128]{2,1,0:T(8,128)(2,1)S(1)}, u32[]{:S(2)}, u32[]{:S(2)}) async-start(bf16[8,96,128]{2,1,0:T(8,128)(2,1)} %get-tuple-element.69), calls=%async_computation.2 | async-start | bytes 393216 | tf_op jit(solution)/shard_map/all_to_all | solution.py:520
  181.8 13.0 %collective-permute-start.19 = (bf16[256,512]{1,0:T(8,128)(2,1)S(1)}, bf16[256,512]{1,0:T(8,128)(2,1)S(1)}, u32[]{:S(2)}, u32[]{:S(2)}) collective-permute-start(bf16[256,512]{1,0:T(8,128)(2,1)S(1)} %br_f.1), channel_id=1, source_target_pairs={{0,4},{2,6},{4,0},{6,2},{1,5},{3,7},{5,1},{7,3},{8,12},{10,14},{12... | collective-permute-start | bytes 786440 | tf_op jit(solution)/shard_map/ppermute | solution.py:57
  185.2 10.5 %collective-permute-start.20 = (bf16[256,512]{1,0:T(8,128)(2,1)S(1)}, bf16[256,512]{1,0:T(8,128)(2,1)S(1)}, u32[]{:S(2)}, u32[]{:S(2)}) collective-permute-start(bf16[256,512]{1,0:T(8,128)(2,1)S(1)} %get-tuple-element.52), channel_id=1, source_target_pairs={{0,2},{2,4},{4,6},{6,0},{1,3},{3,5},{5,7},{7,1},{8,10},{10,12},{12... | collective-permute-start | bytes 786440 | tf_op jit(solution)/shard_map/ppermute | solution.py:57
  190.2 6.7 %collective-permute-start.21 = (bf16[256,512]{1,0:T(8,128)(2,1)S(1)}, bf16[256,512]{1,0:T(8,128)(2,1)S(1)}, u32[]{:S(2)}, u32[]{:S(2)}) collective-permute-start(bf16[256,512]{1,0:T(8,128)(2,1)S(1)} %get-tuple-element.53), channel_id=1, source_target_pairs={{0,6},{2,0},{4,2},{6,4},{1,7},{3,1},{5,3},{7,5},{8,14},{10,8},{12,... | collective-permute-start | bytes 786440 | tf_op jit(solution)/shard_map/ppermute | solution.py:57
  191.4 8.2 %collective-permute-start.28 = (bf16[832,128]{1,0:T(8,128)(2,1)S(1)}, bf16[832,128]{1,0:T(8,128)(2,1)S(1)}, u32[]{:S(2)}, u32[]{:S(2)}) collective-permute-start(bf16[832,128]{1,0:T(8,128)(2,1)S(1)} %pad_maximum_fusion.refs_0_), channel_id=1, source_target_pairs={{0,128},{64,192},{128,0},{192,64},{1,129},{65,193},{129,1},{193,65... | collective-permute-start | bytes 638984 | tf_op jit(solution)/shard_map/ppermute | solution.py:57
  193.0 7.3 %collective-permute-start.27 = (bf16[832,128]{1,0:T(8,128)(2,1)S(1)}, bf16[832,128]{1,0:T(8,128)(2,1)S(1)}, u32[]{:S(2)}, u32[]{:S(2)}) collective-permute-start(bf16[832,128]{1,0:T(8,128)(2,1)S(1)} %pad_maximum_fusion.refs_0_), channel_id=1, source_target_pairs={{0,192},{64,0},{128,64},{192,128},{1,193},{65,1},{129,65},{193,129... | collective-permute-start | bytes 638984 | tf_op jit(solution)/shard_map/ppermute | solution.py:57
  194.8 7.1 %collective-permute-start.26 = (bf16[832,128]{1,0:T(8,128)(2,1)S(1)}, bf16[832,128]{1,0:T(8,128)(2,1)S(1)}, u32[]{:S(2)}, u32[]{:S(2)}) collective-permute-start(bf16[832,128]{1,0:T(8,128)(2,1)S(1)} %pad_maximum_fusion.refs_0_), channel_id=1, source_target_pairs={{0,64},{64,128},{128,192},{192,0},{1,65},{65,129},{129,193},{193,1... | collective-permute-start | bytes 638984 | tf_op jit(solution)/shard_map/ppermute | solution.py:57
  (24 other events, 28.3 us)
Sparse Core Ops, SparseCore 0:
  10.6 99.1 all-gather.1

commit v2 on v1

--- a/solution.py
+++ b/solution.py
@@ -432,7 +432,8 @@
             prod = gab * emb_ref[j, at, :].astype(F32)
             hi = prod.astype(BF)
             low = (prod - hi.astype(F32)).astype(BF)
-            both = dot(hi, expand, NT) + dot(low, expand, NT)
+            both = dot(jnp.concatenate([hi, low], axis=0), expand, NT)
+            both = both[:rows] + both[rows:]
             gattn = jnp.where(group == j, both, gattn)
         attn = attn_ref[at, :]
         gscore = attn * (gattn - over_slots(jnp.add, attn * gattn))
@@ -446,8 +447,8 @@
         gst = jnp.transpose(shi.astype(F32)).astype(BF)
         for j in range(VMAX):
             pick = group2 == j
-            a_w = dot(jnp.where(pick, a2, zero), expand2)
-            s_w = dot(jnp.where(pick, s2, zero), expand2)
+            wide = dot(jnp.concatenate([jnp.where(pick, a2, zero), jnp.where(pick, s2, zero)], axis=0), expand2)
+            a_w, s_w = wide[:rows], wide[rows:]
             ge = (a_w * ga + s_w * qrow).astype(BF)
             mine = slice(16 * j, 16 * j + 16)
             part_q = dot(gst[mine, :], emb_ref[j, at, :])

time: 216 us -> 216 us (level)
  no operation moved by 1% of the time
where the time goes in v2:
time: 216 us; the launch traced here: 213 us
  waiting for transfers between devices  67.1 us (31%)
  Pallas kernels  49 us (23%)
  starting transfers between devices  45.8 us (21%)
  blocking collectives  18.5 us (9%)
  local copies, waits for them, and re-layouts  16.8 us (8%)
  between operations  14.7 us (7%)
    ppermute x6, waiting for transfers between devices, around(): return lax.ppermute(a, (axis, 'c'), steps)  31.8 us
    ppermute x23, starting transfers between devices, send(): return lax.ppermute(a, axis, [(i, (i + k) % n) for i in range(n)])  30.8 us
    ppermute x23, waiting for transfers between devices, send(): return lax.ppermute(a, axis, [(i, (i + k) % n) for i in range(n)])  19.7 us
    all_to_all x1, blocking collectives, gradient_exchange(): got = lax.all_to_all(outs, ('y', 'z'), 0, 0, tiled=True)  18.5 us
    unnamed x82, local copies, waits for them, and re-layouts  15.4 us
    pallas_call x6, Pallas kernels, nt_call(): pl.pallas_call(functools.partial(nt_kernel, steps, other, kept, sums is n...  14.6 us
    all_to_all x1, starting transfers between devices, local(): mine = lax.all_to_all(ordered, ('y', 'z'), 0, 0, tiled=True)  11.4 us
    pallas_call x1, Pallas kernels, up_call(): pl.pallas_call(up_kernel, grid=(n,), out_shape=(sds((NP, HID), F32), sds(...  8.58 us
  transfers between devices with their start and end apart: 32, of which 22 were waited for; matrix products, arithmetic and copies ran while one was open for 1% of the time, Pallas kernels for 17%

profile of v2, /device:TPU:32, one launch (start us, length us, event | category | flops | bytes accessed | tf_op | source)
XLA Modules:
  0.0 212.9 jit_solution(13495496095009003193)
XLA Ops:
  9.3 11.4 %all-to-all-start = ((bf16[32,1,128]{2,1,0:T(2,128)(2,1)}), bf16[32,1,128]{2,1,0:T(2,128)(2,1)S(1)}, u32[]{:S(2)}, u32[]{:S(2)}) async-start(bf16[32,1,128]{2,1,0:T(2,128)(2,1)} %copy.18), calls=%async_computation | async-start | bytes 32768 | tf_op jit(solution)/shard_map/all_to_all | solution.py:551
  21.5 7.8 %all-to-all-done = bf16[32,1,128]{2,1,0:T(2,128)(2,1)S(1)} async-done(((bf16[32,1,128]{2,1,0:T(2,128)(2,1)}), bf16[32,1,128]{2,1,0:T(2,128)(2,1)S(1)}, u32[]{:S(2)}, u32[]{:S(2)}) %all-to-all-start) | async-done | bytes 8224 | tf_op jit(solution)/shard_map/all_to_all | solution.py:551
  29.2 3.0 %collective-permute-start.2 = (bf16[32,128]{1,0:T(8,128)(2,1)S(1)}, bf16[32,128]{1,0:T(8,128)(2,1)S(1)}, u32[]{:S(2)}, u32[]{:S(2)}) collective-permute-start(bf16[32,128]{1,0:T(8,128)(2,1)S(1)} %bitcast.24), channel_id=1, source_target_pairs={{0,4},{2,6},{4,0},{6,2},{1,5},{3,7},{5,1},{7,3},{8,12},{10,14},{12... | collective-permute-start | bytes 24584 | tf_op jit(solution)/shard_map/ppermute | solution.py:57
  32.3 1.1 collective-permute-start.1
  33.4 0.9 collective-permute-start
  34.4 1.5 collective-permute-done.1
  35.9 2.4 %collective-permute-done = bf16[32,128]{1,0:T(8,128)(2,1)S(1)} collective-permute-done((bf16[32,128]{1,0:T(8,128)(2,1)S(1)}, bf16[32,128]{1,0:T(8,128)(2,1)S(1)}, u32[]{:S(2)}, u32[]{:S(2)}) %collective-permute-start) | collective-permute-done | bytes 8224 | tf_op jit(solution)/shard_map/ppermute | solution.py:57
  40.9 1.1 copy-done.12
  43.5 4.6 %attn_fwd.1 = (bf16[272,512]{1,0:T(8,128)(2,1)S(1)}, bf16[8,256,512]{2,1,0:T(8,128)(2,1)S(1)}, f32[256,128]{1,0:T(8,128)S(1)}, bf16[256,128]{1,0:T(8,128)(2,1)S(1)}) custom-call(s32[4]{0:T(128)S(1)} %pad_add_fusion.info, s32[32]{0:T(128)S(1)} %copy-done.8, s32[32]{0:T(128)S(1)} %copy-done.10, s32[256]{0:T(256)S(1)} %reshape.24.var_ids.ids, ...), custom_call_target="tpu_custom_call" | custom-call | flops 805306368 | bytes 4194304 | tf_op jit(solution)/shard_map/attn_fwd/pallas_call | solution.py:150
  48.1 1.3 copy-done.16
  49.6 7.6 %collective-permute-done.5.refs_2_ = bf16[272,512]{1,0:T(8,128)(2,1)S(1)} collective-permute-done((bf16[272,512]{1,0:T(8,128)(2,1)S(1)}, bf16[272,512]{1,0:T(8,128)(2,1)S(1)}, u32[]{:S(2)}, u32[]{:S(2)}) %collective-permute-start.5) | collective-permute-done | bytes 278560 | tf_op jit(solution)/shard_map/ppermute | solution.py:63
  57.4 7.5 %collective-permute-done.7.refs_4_ = bf16[272,512]{1,0:T(8,128)(2,1)S(1)} collective-permute-done((bf16[272,512]{1,0:T(8,128)(2,1)S(1)}, bf16[272,512]{1,0:T(8,128)(2,1)S(1)}, u32[]{:S(2)}, u32[]{:S(2)}) %collective-permute-start.7) | collective-permute-done | bytes 278560 | tf_op jit(solution)/shard_map/ppermute | solution.py:63
  64.9 3.0 %collective-permute-done.6.refs_3_ = bf16[272,512]{1,0:T(8,128)(2,1)S(1)} collective-permute-done((bf16[272,512]{1,0:T(8,128)(2,1)S(1)}, bf16[272,512]{1,0:T(8,128)(2,1)S(1)}, u32[]{:S(2)}, u32[]{:S(2)}) %collective-permute-start.6) | collective-permute-done | bytes 278560 | tf_op jit(solution)/shard_map/ppermute | solution.py:63
  68.2 1.5 collective-permute-done.9.refs_6_
  70.5 8.6 %ln_up.1 = (f32[256,1024]{1,0:T(8,128)S(1)}, f32[256,1024]{1,0:T(8,128)S(1)}, bf16[256,1024]{1,0:T(8,128)(2,1)S(1)}, f32[8,1024]{1,0:T(8,128)S(1)}, f32[2,256,128]{2,1,0:T(8,128)S(1)}) custom-call(s32[4]{0:T(128)S(1)} %pad_add_fusion.info, bf16[272,512]{1,0:T(8,128)(2,1)} %copy-done.4, bf16[272,512]{1,0:T(8,128)(2,1)} %copy-done.19, ...), custom_call_target="tpu_custom_call" | custom-call | flops 2281701376 | bytes 16777216 | tf_op jit(solution)/shard_map/ln_up/pallas_call | solution.py:219
  79.1 1.0 copy-done.6
  80.1 1.4 collective-permute-done.13.refs_1_
  81.6 6.1 %collective-permute-done.11.refs_2_ = bf16[256,512]{1,0:T(8,128)(2,1)S(1)} collective-permute-done((bf16[256,512]{1,0:T(8,128)(2,1)S(1)}, bf16[256,512]{1,0:T(8,128)(2,1)S(1)}, u32[]{:S(2)}, u32[]{:S(2)}) %collective-permute-start.11) | collective-permute-done | bytes 262176 | tf_op jit(solution)/shard_map/ppermute | solution.py:63
  87.7 2.8 %collective-permute-done.14.refs_3_ = bf16[256,512]{1,0:T(8,128)(2,1)S(1)} collective-permute-done((bf16[256,512]{1,0:T(8,128)(2,1)S(1)}, bf16[256,512]{1,0:T(8,128)(2,1)S(1)}, u32[]{:S(2)}, u32[]{:S(2)}) %collective-permute-start.14) | collective-permute-done | bytes 262176 | tf_op jit(solution)/shard_map/ppermute | solution.py:63
  90.5 4.8 %collective-permute-done.12.refs_4_ = bf16[256,512]{1,0:T(8,128)(2,1)S(1)} collective-permute-done((bf16[256,512]{1,0:T(8,128)(2,1)S(1)}, bf16[256,512]{1,0:T(8,128)(2,1)S(1)}, u32[]{:S(2)}, u32[]{:S(2)}) %collective-permute-start.12) | collective-permute-done | bytes 262176 | tf_op jit(solution)/shard_map/ppermute | solution.py:63
  96.1 3.3 %copy-done.1 = bf16[4096,1024]{1,0:T(8,128)(2,1)} copy-done((bf16[4096,1024]{1,0:T(8,128)(2,1)}, bf16[4096,1024]{1,0:T(8,128)(2,1)S(1)}, u32[]{:S(2)}) %copy-start.1) | copy-done | bytes 8388632
  100.9 1.7 join.1.g
  102.6 7.2 %all-gather.2.cloned.1.call-done.rhs_ref.down_ref = bf16[4096,1024]{1,0:T(8,128)(2,1)} async-done(((bf16[128,1024]{1,0:T(8,128)(2,1)}), bf16[4096,1024]{1,0:T(8,128)(2,1)}) %all-gather.2.cloned.1.call-update) | async-done | bytes 8388624 | tf_op jit(solution)/shard_map/all_gather | solution.py:547
  109.8 5.7 %grad_pre.1 = (bf16[256,1024]{1,0:T(8,128)(2,1)S(1)}, bf16[16,512]{1,0:T(8,128)(2,1)S(1)}) custom-call(bf16[256,4096]{1,0:T(8,128)(2,1)S(1)} %join.1.g, bf16[4096,1024]{1,0:T(8,128)(2,1)} %all-gather.2.cloned.1.call-done.rhs_ref.down_ref, f32[256,1024]{1,0:T(8,128)} %copy-done.6, f32[256,1024]{1,0:T(8,128)} %copy-done.7, f32[8,1024]{1,0:T(8,128)S(1)} %get-tuple-element.44.u_ref), custom_call_target="tpu_custom_call" | custom-call | flops 2147483648 | bytes 12582912 | tf_op jit(solution)/shard_map/grad_pre/pallas_call | solution.py:291
  116.3 1.8 gn_o.1
  118.2 2.7 %collective-permute-done.22.refs_1_ = bf16[4,272,512]{2,1,0:T(8,128)(2,1)S(1)} collective-permute-done((bf16[4,272,512]{2,1,0:T(8,128)(2,1)S(1)}, bf16[4,272,512]{2,1,0:T(8,128)(2,1)S(1)}, u32[]{:S(2)}, u32[]{:S(2)}) %collective-permute-start.22) | collective-permute-done | bytes 1114144 | tf_op jit(solution)/shard_map/ppermute | solution.py:57
  121.0 1.0 gn_f.1
  122.0 1.6 gn_n.1
  123.6 1.5 collective-permute-start.24
  125.1 11.7 %collective-permute-start.25 = (bf16[272,512]{1,0:T(8,128)(2,1)S(1)}, bf16[272,512]{1,0:T(8,128)(2,1)S(1)}, u32[]{:S(2)}, u32[]{:S(2)}) collective-permute-start(bf16[272,512]{1,0:T(8,128)(2,1)S(1)} %get-tuple-element.64), channel_id=1, source_target_pairs={{0,6},{2,0},{4,2},{6,4},{1,7},{3,1},{5,3},{7,5},{8,14},{10,8},{12,... | collective-permute-start | bytes 835592 | tf_op jit(solution)/shard_map/ppermute | solution.py:57
  136.8 1.8 collective-permute-start.23
  138.6 4.7 %br_o.1 = bf16[4,256,512]{2,1,0:T(8,128)(2,1)} custom-call(s32[4]{0:T(128)S(1)} %pad_add_fusion.info, bf16[256,1024]{1,0:T(8,128)(2,1)S(1)} %get-tuple-element.49.lhs_ref, bf16[4096,1024]{1,0:T(8,128)(2,1)} %all-gather.2.cloned.1.call-done.rhs_ref.down_ref), custom_call_target="tpu_custom_call" | custom-call | flops 1073741824 | bytes 4194304 | tf_op jit(solution)/shard_map/br_o/pallas_call | solution.py:367
  143.3 3.2 %collective-permute-done.23.b_ref = bf16[272,512]{1,0:T(8,128)(2,1)S(1)} collective-permute-done((bf16[272,512]{1,0:T(8,128)(2,1)S(1)}, bf16[272,512]{1,0:T(8,128)(2,1)S(1)}, u32[]{:S(2)}, u32[]{:S(2)}) %collective-permute-start.23) | collective-permute-done | bytes 278560 | tf_op jit(solution)/shard_map/ppermute | solution.py:57
  146.7 2.2 %collective-permute-done.25.p2_ref = bf16[272,512]{1,0:T(8,128)(2,1)S(1)} collective-permute-done((bf16[272,512]{1,0:T(8,128)(2,1)S(1)}, bf16[272,512]{1,0:T(8,128)(2,1)S(1)}, u32[]{:S(2)}, u32[]{:S(2)}) %collective-permute-start.25) | collective-permute-done | bytes 278560 | tf_op jit(solution)/shard_map/ppermute | solution.py:57
  149.6 5.5 %attn_bwd.1 = bf16[32,32,128]{2,1,0:T(8,128)(2,1)S(1)} custom-call(f32[272,512]{1,0:T(8,128)S(1)} %gn_p.1.own_ref, bf16[272,512]{1,0:T(8,128)(2,1)} %copy-done.38, bf16[272,512]{1,0:T(8,128)(2,1)} %copy-done.39, bf16[272,512]{1,0:T(8,128)(2,1)S(1)} %copy-done.5, f32[2,256,128]{2,1,0:T(8,128)S(1)} %get-tuple-element.65.st_ref, bf16[1,512]{1,0:T(2,128)(2,1)S(1)} %copy-done.15, ...), custom_call_target="tpu_custom_call" | custom-call | flops 1610612736 | bytes 5242880 | tf_op jit(solution)/shard_map/attn_bwd/pallas_call | solution.py:471
  155.1 18.5 %all_to_all.22.got_ref = bf16[32,32,128]{2,1,0:T(8,128)(2,1)S(1)} all-to-all(bf16[32,32,128]{2,1,0:T(8,128)(2,1)S(1)} %attn_bwd.1), channel_id=1, replica_groups=mesh['y'=4,'z'=8,'x'=4,'c'=2] {'y','z'}, dimensions={0} | all-to-all | bytes 524288 | tf_op jit(solution)/shard_map/all_to_all | solution.py:514
  173.6 2.4 %slot_sum.1 = (bf16[8,96,128]{2,1,0:T(8,128)(2,1)}, bf16[64,128]{1,0:T(8,128)(2,1)S(1)}) custom-call(s32[32]{0:T(128)S(1)} %copy-done.9, s32[32]{0:T(128)S(1)} %copy-done.11, s32[256]{0:T(256)S(1)} %reshape.24.var_ids.ids, bf16[32,32,128]{2,1,0:T(8,128)(2,1)S(1)} %all_to_all.22.got_ref), custom_call_target="tpu_custom_call" | custom-call | flops 1048576 | bytes 2097152 | tf_op jit(solution)/shard_map/slot_sum/pallas_call | solution.py:515
  176.0 3.5 %all-to-all-start.2 = ((bf16[8,96,128]{2,1,0:T(8,128)(2,1)}), bf16[8,96,128]{2,1,0:T(8,128)(2,1)S(1)}, u32[]{:S(2)}, u32[]{:S(2)}) async-start(bf16[8,96,128]{2,1,0:T(8,128)(2,1)} %get-tuple-element.69), calls=%async_computation.2 | async-start | bytes 393216 | tf_op jit(solution)/shard_map/all_to_all | solution.py:521
  179.5 2.3 %br_f.1 = bf16[256,512]{1,0:T(8,128)(2,1)S(1)} custom-call(s32[4]{0:T(128)S(1)} %pad_add_fusion.info, bf16[256,1024]{1,0:T(8,128)(2,1)S(1)} %get-tuple-element.49.lhs_ref, bf16[4096,1024]{1,0:T(8,128)(2,1)} %all-gather.2.cloned.1.call-done.rhs_ref.down_ref, bf16[4,256,512]{2,1,0:T(8,128)(2,1)S(1)} %collective-permute-done.18.refs_0_), custom_call_target="tpu_custom_call" | custom-call | flops 268435456 | bytes 1048576 | tf_op jit(solution)/shard_map/br_f/pallas_call | solution.py:367
  181.9 3.2 %br_n.1 = (bf16[256,512]{1,0:T(8,128)(2,1)S(1)}, bf16[256,512]{1,0:T(8,128)(2,1)S(1)}, bf16[256,512]{1,0:T(8,128)(2,1)S(1)}) custom-call(s32[4]{0:T(128)S(1)} %pad_add_fusion.info, bf16[256,1024]{1,0:T(8,128)(2,1)S(1)} %get-tuple-element.49.lhs_ref, bf16[4096,1024]{1,0:T(8,128)(2,1)} %all-gather.2.cloned.1.call-done.rhs_ref.down_ref, ...), custom_call_target="tpu_custom_call" | custom-call | flops 805306368 | bytes 3145728 | tf_op jit(solution)/shard_map/br_n/pallas_call | solution.py:367
  185.1 5.0 %collective-permute-start.20 = (bf16[256,512]{1,0:T(8,128)(2,1)S(1)}, bf16[256,512]{1,0:T(8,128)(2,1)S(1)}, u32[]{:S(2)}, u32[]{:S(2)}) collective-permute-start(bf16[256,512]{1,0:T(8,128)(2,1)S(1)} %get-tuple-element.52), channel_id=1, source_target_pairs={{0,2},{2,4},{4,6},{6,0},{1,3},{3,5},{5,7},{7,1},{8,10},{10,12},{12... | collective-permute-start | bytes 786440 | tf_op jit(solution)/shard_map/ppermute | solution.py:57
  190.1 1.2 collective-permute-start.21
  191.4 1.6 collective-permute-start.28
  193.0 1.8 collective-permute-start.27
  195.6 1.2 collective-permute-done.21.p2
  197.5 1.8 mix.1
  200.3 1.5 collective-permute-done.26.refs_1_
  202.6 3.3 %spread.1 = (f32[48,16,512]{2,1,0:T(8,128)}, f32[48,512]{1,0:T(8,128)}, f32[1,512]{1,0:T(1,128)}) custom-call(s32[4]{0:T(128)S(1)} %pad_add_fusion.info, bf16[832,128]{1,0:T(8,128)(2,1)S(1)} %pad_maximum_fusion.refs_0_, bf16[832,128]{1,0:T(8,128)(2,1)} %copy-done.37, bf16[832,128]{1,0:T(8,128)(2,1)} %copy-done.36, bf16[832,128]{1,0:T(8,128)(2,1)} %copy-done.35), custom_call_target="tpu_custom_call" | custom-call | flops 1048576 | bytes 3145728 | tf_op jit(solution)/shard_map/spread/pallas_call | solution.py:524
  (125 shorter events, 16.0 us)
Async XLA Ops:
  7.2 102.7 %all-gather.2.cloned.1.call-start = ((), (), s32[]{:S(2)}) async-start(), calls=%async_computation.3 | async-start | bytes 8650752 | tf_op jit(solution)/shard_map/all_gather | solution.py:547
  9.3 19.9 %all-to-all-start = ((bf16[32,1,128]{2,1,0:T(2,128)(2,1)}), bf16[32,1,128]{2,1,0:T(2,128)(2,1)S(1)}, u32[]{:S(2)}, u32[]{:S(2)}) async-start(bf16[32,1,128]{2,1,0:T(2,128)(2,1)} %copy.18), calls=%async_computation | async-start | bytes 32768 | tf_op jit(solution)/shard_map/all_to_all | solution.py:551
  29.2 5.2 %collective-permute-start.2 = (bf16[32,128]{1,0:T(8,128)(2,1)S(1)}, bf16[32,128]{1,0:T(8,128)(2,1)S(1)}, u32[]{:S(2)}, u32[]{:S(2)}) collective-permute-start(bf16[32,128]{1,0:T(8,128)(2,1)S(1)} %bitcast.24), channel_id=1, source_target_pairs={{0,4},{2,6},{4,0},{6,2},{1,5},{3,7},{5,1},{7,3},{8,12},{10,14},{12... | collective-permute-start | bytes 24584 | tf_op jit(solution)/shard_map/ppermute | solution.py:57
  32.3 3.7 %collective-permute-start.1 = (bf16[32,128]{1,0:T(8,128)(2,1)S(1)}, bf16[32,128]{1,0:T(8,128)(2,1)S(1)}, u32[]{:S(2)}, u32[]{:S(2)}) collective-permute-start(bf16[32,128]{1,0:T(8,128)(2,1)S(1)} %bitcast.25), channel_id=1, source_target_pairs={{0,6},{2,0},{4,2},{6,4},{1,7},{3,1},{5,3},{7,5},{8,14},{10,8},{12,... | collective-permute-start | bytes 24584 | tf_op jit(solution)/shard_map/ppermute | solution.py:57
  33.4 4.9 %collective-permute-start = (bf16[32,128]{1,0:T(8,128)(2,1)S(1)}, bf16[32,128]{1,0:T(8,128)(2,1)S(1)}, u32[]{:S(2)}, u32[]{:S(2)}) collective-permute-start(bf16[32,128]{1,0:T(8,128)(2,1)S(1)} %bitcast.26), channel_id=1, source_target_pairs={{0,2},{2,4},{4,6},{6,0},{1,3},{3,5},{5,7},{7,1},{8,10},{10,12},{12... | collective-permute-start | bytes 24584 | tf_op jit(solution)/shard_map/ppermute | solution.py:57
  38.3 1.3 collective-permute-start.3
  49.4 20.3 %copy-start.4 = (bf16[272,512]{1,0:T(8,128)(2,1)}, bf16[272,512]{1,0:T(8,128)(2,1)S(1)}, u32[]{:S(2)}) copy-start(bf16[272,512]{1,0:T(8,128)(2,1)S(1)} %get-tuple-element.42.refs_0_.agg_ref) | copy-start | bytes 835588
  49.4 30.6 %copy-start.25 = (bf16[1,256,512]{2,1,0:T(8,128)(2,1)S(1)}, bf16[1,256,512]{2,1,0:T(8,128)(2,1)}, u32[]{:S(2)}) copy-start(bf16[1,256,512]{2,1,0:T(8,128)(2,1)} %param.21) | copy-start | bytes 786436
  49.4 7.8 %collective-permute-start.5 = (bf16[272,512]{1,0:T(8,128)(2,1)S(1)}, bf16[272,512]{1,0:T(8,128)(2,1)S(1)}, u32[]{:S(2)}, u32[]{:S(2)}) collective-permute-start(bf16[272,512]{1,0:T(8,128)(2,1)S(1)} %get-tuple-element.42.refs_0_.agg_ref), channel_id=1, source_target_pairs={{0,2},{1,7},{2,4},{3,1},{4,6},{5,3},{6,0},{7,5},{8,10},{9,15},{10,... | collective-permute-start | bytes 835592 | tf_op jit(solution)/shard_map/ppermute | solution.py:63
  49.4 7.8 %collective-permute-start.4 = (bf16[272,512]{1,0:T(8,128)(2,1)S(1)}, bf16[272,512]{1,0:T(8,128)(2,1)S(1)}, u32[]{:S(2)}, u32[]{:S(2)}) collective-permute-start(bf16[272,512]{1,0:T(8,128)(2,1)S(1)} %get-tuple-element.42.refs_0_.agg_ref), channel_id=1, source_target_pairs={{0,1},{1,0},{2,3},{3,2},{4,5},{5,4},{6,7},{7,6},{8,9},{9,8},{10,11... | collective-permute-start | bytes 835592 | tf_op jit(solution)/shard_map/ppermute | solution.py:57
  57.2 12.5 %copy-start.18 = (bf16[272,512]{1,0:T(8,128)(2,1)}, bf16[272,512]{1,0:T(8,128)(2,1)S(1)}, u32[]{:S(2)}) copy-start(bf16[272,512]{1,0:T(8,128)(2,1)S(1)} %collective-permute-done.5.refs_2_) | copy-start | bytes 835588
  57.2 7.8 %collective-permute-start.7 = (bf16[272,512]{1,0:T(8,128)(2,1)S(1)}, bf16[272,512]{1,0:T(8,128)(2,1)S(1)}, u32[]{:S(2)}, u32[]{:S(2)}) collective-permute-start(bf16[272,512]{1,0:T(8,128)(2,1)S(1)} %collective-permute-done.5.refs_2_), channel_id=1, source_target_pairs={{0,2},{1,7},{2,4},{3,1},{4,6},{5,3},{6,0},{7,5},{8,10},{9,15},{10,... | collective-permute-start | bytes 835592 | tf_op jit(solution)/shard_map/ppermute | solution.py:63
  57.2 12.5 %copy-start.19 = (bf16[272,512]{1,0:T(8,128)(2,1)}, bf16[272,512]{1,0:T(8,128)(2,1)S(1)}, u32[]{:S(2)}) copy-start(bf16[272,512]{1,0:T(8,128)(2,1)S(1)} %collective-permute-done.4.refs_1_) | copy-start | bytes 835588
  57.2 10.7 %collective-permute-start.6 = (bf16[272,512]{1,0:T(8,128)(2,1)S(1)}, bf16[272,512]{1,0:T(8,128)(2,1)S(1)}, u32[]{:S(2)}, u32[]{:S(2)}) collective-permute-start(bf16[272,512]{1,0:T(8,128)(2,1)S(1)} %collective-permute-done.4.refs_1_), channel_id=1, source_target_pairs={{0,2},{1,7},{2,4},{3,1},{4,6},{5,3},{6,0},{7,5},{8,10},{9,15},{10,... | collective-permute-start | bytes 835592 | tf_op jit(solution)/shard_map/ppermute | solution.py:63
  57.3 10.9 %collective-permute-start.8 = (bf16[272,512]{1,0:T(8,128)(2,1)S(1)}, bf16[272,512]{1,0:T(8,128)(2,1)S(1)}, u32[]{:S(2)}, u32[]{:S(2)}) collective-permute-start(bf16[272,512]{1,0:T(8,128)(2,1)S(1)} %collective-permute-done.5.refs_2_), channel_id=1, source_target_pairs={{0,1},{1,0},{2,3},{3,2},{4,5},{5,4},{6,7},{7,6},{8,9},{9,8},{10,11... | collective-permute-start | bytes 835592 | tf_op jit(solution)/shard_map/ppermute | solution.py:57
  64.9 4.8 %copy-start.20 = (bf16[272,512]{1,0:T(8,128)(2,1)}, bf16[272,512]{1,0:T(8,128)(2,1)S(1)}, u32[]{:S(2)}) copy-start(bf16[272,512]{1,0:T(8,128)(2,1)S(1)} %collective-permute-done.7.refs_4_) | copy-start | bytes 835588
  64.9 3.3 %collective-permute-start.10 = (bf16[272,512]{1,0:T(8,128)(2,1)S(1)}, bf16[272,512]{1,0:T(8,128)(2,1)S(1)}, u32[]{:S(2)}, u32[]{:S(2)}) collective-permute-start(bf16[272,512]{1,0:T(8,128)(2,1)S(1)} %collective-permute-done.7.refs_4_), channel_id=1, source_target_pairs={{0,1},{1,0},{2,3},{3,2},{4,5},{5,4},{6,7},{7,6},{8,9},{9,8},{10,11... | collective-permute-start | bytes 835592 | tf_op jit(solution)/shard_map/ppermute | solution.py:57
  67.9 1.8 collective-permute-start.9
  70.5 25.0 %copy-start.3 = (bf16[4096,1024]{1,0:T(8,128)(2,1)S(1)}, bf16[4096,1024]{1,0:T(8,128)(2,1)}, u32[]{:S(2)}) copy-start(bf16[4096,1024]{1,0:T(8,128)(2,1)} %src) | copy-start | bytes 25165828
  80.0 16.0 %copy-start.7 = (f32[256,1024]{1,0:T(8,128)}, f32[256,1024]{1,0:T(8,128)S(1)}, u32[]{:S(2)}) copy-start(f32[256,1024]{1,0:T(8,128)S(1)} %get-tuple-element.56.dg_ref) | copy-start | bytes 3145732
  80.0 1.5 collective-permute-start.13
  80.1 7.6 %collective-permute-start.11 = (bf16[256,512]{1,0:T(8,128)(2,1)S(1)}, bf16[256,512]{1,0:T(8,128)(2,1)S(1)}, u32[]{:S(2)}, u32[]{:S(2)}) collective-permute-start(bf16[256,512]{1,0:T(8,128)(2,1)S(1)} %bitcast.23), channel_id=1, source_target_pairs={{0,2},{1,7},{2,4},{3,1},{4,6},{5,3},{6,0},{7,5},{8,10},{9,15},{10,... | collective-permute-start | bytes 786440 | tf_op jit(solution)/shard_map/ppermute | solution.py:63
  81.6 14.5 %copy-start.26 = (bf16[256,512]{1,0:T(8,128)(2,1)}, bf16[256,512]{1,0:T(8,128)(2,1)S(1)}, u32[]{:S(2)}) copy-start(bf16[256,512]{1,0:T(8,128)(2,1)S(1)} %collective-permute-done.13.refs_1_) | copy-start | bytes 786436
  81.6 8.9 %collective-permute-start.14 = (bf16[256,512]{1,0:T(8,128)(2,1)S(1)}, bf16[256,512]{1,0:T(8,128)(2,1)S(1)}, u32[]{:S(2)}, u32[]{:S(2)}) collective-permute-start(bf16[256,512]{1,0:T(8,128)(2,1)S(1)} %collective-permute-done.13.refs_1_), channel_id=1, source_target_pairs={{0,2},{1,7},{2,4},{3,1},{4,6},{5,3},{6,0},{7,5},{8,10},{9,15},{10,... | collective-permute-start | bytes 786440 | tf_op jit(solution)/shard_map/ppermute | solution.py:63
  87.7 8.4 %copy-start.27 = (bf16[256,512]{1,0:T(8,128)(2,1)}, bf16[256,512]{1,0:T(8,128)(2,1)S(1)}, u32[]{:S(2)}) copy-start(bf16[256,512]{1,0:T(8,128)(2,1)S(1)} %collective-permute-done.11.refs_2_) | copy-start | bytes 786436
  87.7 7.6 %collective-permute-start.12 = (bf16[256,512]{1,0:T(8,128)(2,1)S(1)}, bf16[256,512]{1,0:T(8,128)(2,1)S(1)}, u32[]{:S(2)}, u32[]{:S(2)}) collective-permute-start(bf16[256,512]{1,0:T(8,128)(2,1)S(1)} %collective-permute-done.11.refs_2_), channel_id=1, source_target_pairs={{0,2},{1,7},{2,4},{3,1},{4,6},{5,3},{6,0},{7,5},{8,10},{9,15},{10,... | collective-permute-start | bytes 786440 | tf_op jit(solution)/shard_map/ppermute | solution.py:63
  87.7 11.7 %collective-permute-start.15 = (bf16[256,512]{1,0:T(8,128)(2,1)S(1)}, bf16[256,512]{1,0:T(8,128)(2,1)S(1)}, u32[]{:S(2)}, u32[]{:S(2)}) collective-permute-start(bf16[256,512]{1,0:T(8,128)(2,1)S(1)} %collective-permute-done.11.refs_2_), channel_id=1, source_target_pairs={{0,1},{1,0},{2,3},{3,2},{4,5},{5,4},{6,7},{7,6},{8,9},{9,8},{10,11... | collective-permute-start | bytes 786440 | tf_op jit(solution)/shard_map/ppermute | solution.py:57
  90.5 5.6 %copy-start.29 = (bf16[256,512]{1,0:T(8,128)(2,1)}, bf16[256,512]{1,0:T(8,128)(2,1)S(1)}, u32[]{:S(2)}) copy-start(bf16[256,512]{1,0:T(8,128)(2,1)S(1)} %collective-permute-done.14.refs_3_) | copy-start | bytes 786436
  90.5 8.9 %collective-permute-start.16 = (bf16[256,512]{1,0:T(8,128)(2,1)S(1)}, bf16[256,512]{1,0:T(8,128)(2,1)S(1)}, u32[]{:S(2)}, u32[]{:S(2)}) collective-permute-start(bf16[256,512]{1,0:T(8,128)(2,1)S(1)} %collective-permute-done.14.refs_3_), channel_id=1, source_target_pairs={{0,1},{1,0},{2,3},{3,2},{4,5},{5,4},{6,7},{7,6},{8,9},{9,8},{10,11... | collective-permute-start | bytes 786440 | tf_op jit(solution)/shard_map/ppermute | solution.py:57
  95.3 4.2 %collective-permute-start.17 = (bf16[256,512]{1,0:T(8,128)(2,1)S(1)}, bf16[256,512]{1,0:T(8,128)(2,1)S(1)}, u32[]{:S(2)}, u32[]{:S(2)}) collective-permute-start(bf16[256,512]{1,0:T(8,128)(2,1)S(1)} %collective-permute-done.12.refs_4_), channel_id=1, source_target_pairs={{0,1},{1,0},{2,3},{3,2},{4,5},{5,4},{6,7},{7,6},{8,9},{9,8},{10,11... | collective-permute-start | bytes 786440 | tf_op jit(solution)/shard_map/ppermute | solution.py:57
  109.8 6.5 %copy-start.2 = (bf16[4096,1024]{1,0:T(8,128)(2,1)S(1)}, bf16[4096,1024]{1,0:T(8,128)(2,1)}, u32[]{:S(2)}) copy-start(bf16[4096,1024]{1,0:T(8,128)(2,1)} %copy-done.1) | copy-start | bytes 25165828
  118.1 2.8 %collective-permute-start.22 = (bf16[4,272,512]{2,1,0:T(8,128)(2,1)S(1)}, bf16[4,272,512]{2,1,0:T(8,128)(2,1)S(1)}, u32[]{:S(2)}, u32[]{:S(2)}) collective-permute-start(bf16[4,272,512]{2,1,0:T(8,128)(2,1)S(1)} %gn_o.1), channel_id=1, source_target_pairs={{0,1},{1,0},{2,3},{3,2},{4,5},{5,4},{6,7},{7,6},{8,9},{9,8},{10,11... | collective-permute-start | bytes 3342344 | tf_op jit(solution)/shard_map/ppermute | solution.py:57
  123.6 23.1 %collective-permute-start.24 = (bf16[272,512]{1,0:T(8,128)(2,1)S(1)}, bf16[272,512]{1,0:T(8,128)(2,1)S(1)}, u32[]{:S(2)}, u32[]{:S(2)}) collective-permute-start(bf16[272,512]{1,0:T(8,128)(2,1)S(1)} %get-tuple-element.63), channel_id=1, source_target_pairs={{0,2},{2,4},{4,6},{6,0},{1,3},{3,5},{5,7},{7,1},{8,10},{10,12},{12... | collective-permute-start | bytes 835592 | tf_op jit(solution)/shard_map/ppermute | solution.py:57
  125.1 24.5 %copy-start.5 = (bf16[272,512]{1,0:T(8,128)(2,1)S(1)}, bf16[272,512]{1,0:T(8,128)(2,1)}, u32[]{:S(2)}) copy-start(bf16[272,512]{1,0:T(8,128)(2,1)} %copy-done.4) | copy-start | bytes 835588
  125.1 24.5 %copy-start.15 = (bf16[1,512]{1,0:T(2,128)(2,1)S(1)}, bf16[1,512]{1,0:T(2,128)(2,1)}, u32[]{:S(2)}) copy-start(bf16[1,512]{1,0:T(2,128)(2,1)} %gain_ref.3) | copy-start | bytes 3076
  125.1 24.5 %copy-start.17 = (bf16[8,256,512]{2,1,0:T(8,128)(2,1)S(1)}, bf16[8,256,512]{2,1,0:T(8,128)(2,1)}, u32[]{:S(2)}) copy-start(bf16[8,256,512]{2,1,0:T(8,128)(2,1)} %copy-done.16) | copy-start | bytes 6291460
  125.1 23.7 %collective-permute-start.25 = (bf16[272,512]{1,0:T(8,128)(2,1)S(1)}, bf16[272,512]{1,0:T(8,128)(2,1)S(1)}, u32[]{:S(2)}, u32[]{:S(2)}) collective-permute-start(bf16[272,512]{1,0:T(8,128)(2,1)S(1)} %get-tuple-element.64), channel_id=1, source_target_pairs={{0,6},{2,0},{4,2},{6,4},{1,7},{3,1},{5,3},{7,5},{8,14},{10,8},{12,... | collective-permute-start | bytes 835592 | tf_op jit(solution)/shard_map/ppermute | solution.py:57
  136.8 9.8 %collective-permute-start.23 = (bf16[272,512]{1,0:T(8,128)(2,1)S(1)}, bf16[272,512]{1,0:T(8,128)(2,1)S(1)}, u32[]{:S(2)}, u32[]{:S(2)}) collective-permute-start(bf16[272,512]{1,0:T(8,128)(2,1)S(1)} %gn_f.1), channel_id=1, source_target_pairs={{0,4},{2,6},{4,0},{6,2},{1,5},{3,7},{5,1},{7,3},{8,12},{10,14},{12... | collective-permute-start | bytes 835592 | tf_op jit(solution)/shard_map/ppermute | solution.py:57
  143.2 36.3 %collective-permute-start.18 = (bf16[4,256,512]{2,1,0:T(8,128)(2,1)}, bf16[4,256,512]{2,1,0:T(8,128)(2,1)S(1)}, u32[]{:S(2)}, u32[]{:S(2)}) collective-permute-start(bf16[4,256,512]{2,1,0:T(8,128)(2,1)} %br_o.1), channel_id=1, source_target_pairs={{0,1},{1,0},{2,3},{3,2},{4,5},{5,4},{6,7},{7,6},{8,9},{9,8},{10,11... | collective-permute-start | bytes 3145736 | tf_op jit(solution)/shard_map/ppermute | solution.py:57
  149.6 24.0 %copy-start.9 = (s32[32]{0:T(128)S(1)}, s32[32]{0:T(128)}, u32[]{:S(2)}) copy-start(s32[32]{0:T(128)} %destination.3) | copy-start | bytes 388
  149.6 24.0 %copy-start.11 = (s32[32]{0:T(128)S(1)}, s32[32]{0:T(128)}, u32[]{:S(2)}) copy-start(s32[32]{0:T(128)} %counts.3) | copy-start | bytes 388
  176.0 15.3 %all-to-all-start.2 = ((bf16[8,96,128]{2,1,0:T(8,128)(2,1)}), bf16[8,96,128]{2,1,0:T(8,128)(2,1)S(1)}, u32[]{:S(2)}, u32[]{:S(2)}) async-start(bf16[8,96,128]{2,1,0:T(8,128)(2,1)} %get-tuple-element.69), calls=%async_computation.2 | async-start | bytes 393216 | tf_op jit(solution)/shard_map/all_to_all | solution.py:521
  181.8 13.0 %collective-permute-start.19 = (bf16[256,512]{1,0:T(8,128)(2,1)S(1)}, bf16[256,512]{1,0:T(8,128)(2,1)S(1)}, u32[]{:S(2)}, u32[]{:S(2)}) collective-permute-start(bf16[256,512]{1,0:T(8,128)(2,1)S(1)} %br_f.1), channel_id=1, source_target_pairs={{0,4},{2,6},{4,0},{6,2},{1,5},{3,7},{5,1},{7,3},{8,12},{10,14},{12... | collective-permute-start | bytes 786440 | tf_op jit(solution)/shard_map/ppermute | solution.py:57
  185.1 10.5 %collective-permute-start.20 = (bf16[256,512]{1,0:T(8,128)(2,1)S(1)}, bf16[256,512]{1,0:T(8,128)(2,1)S(1)}, u32[]{:S(2)}, u32[]{:S(2)}) collective-permute-start(bf16[256,512]{1,0:T(8,128)(2,1)S(1)} %get-tuple-element.52), channel_id=1, source_target_pairs={{0,2},{2,4},{4,6},{6,0},{1,3},{3,5},{5,7},{7,1},{8,10},{10,12},{12... | collective-permute-start | bytes 786440 | tf_op jit(solution)/shard_map/ppermute | solution.py:57
  190.1 6.7 %collective-permute-start.21 = (bf16[256,512]{1,0:T(8,128)(2,1)S(1)}, bf16[256,512]{1,0:T(8,128)(2,1)S(1)}, u32[]{:S(2)}, u32[]{:S(2)}) collective-permute-start(bf16[256,512]{1,0:T(8,128)(2,1)S(1)} %get-tuple-element.53), channel_id=1, source_target_pairs={{0,6},{2,0},{4,2},{6,4},{1,7},{3,1},{5,3},{7,5},{8,14},{10,8},{12,... | collective-permute-start | bytes 786440 | tf_op jit(solution)/shard_map/ppermute | solution.py:57
  191.4 8.2 %collective-permute-start.28 = (bf16[832,128]{1,0:T(8,128)(2,1)S(1)}, bf16[832,128]{1,0:T(8,128)(2,1)S(1)}, u32[]{:S(2)}, u32[]{:S(2)}) collective-permute-start(bf16[832,128]{1,0:T(8,128)(2,1)S(1)} %pad_maximum_fusion.refs_0_), channel_id=1, source_target_pairs={{0,128},{64,192},{128,0},{192,64},{1,129},{65,193},{129,1},{193,65... | collective-permute-start | bytes 638984 | tf_op jit(solution)/shard_map/ppermute | solution.py:57
  193.0 7.3 %collective-permute-start.27 = (bf16[832,128]{1,0:T(8,128)(2,1)S(1)}, bf16[832,128]{1,0:T(8,128)(2,1)S(1)}, u32[]{:S(2)}, u32[]{:S(2)}) collective-permute-start(bf16[832,128]{1,0:T(8,128)(2,1)S(1)} %pad_maximum_fusion.refs_0_), channel_id=1, source_target_pairs={{0,192},{64,0},{128,64},{192,128},{1,193},{65,1},{129,65},{193,129... | collective-permute-start | bytes 638984 | tf_op jit(solution)/shard_map/ppermute | solution.py:57
  194.8 7.1 %collective-permute-start.26 = (bf16[832,128]{1,0:T(8,128)(2,1)S(1)}, bf16[832,128]{1,0:T(8,128)(2,1)S(1)}, u32[]{:S(2)}, u32[]{:S(2)}) collective-permute-start(bf16[832,128]{1,0:T(8,128)(2,1)S(1)} %pad_maximum_fusion.refs_0_), channel_id=1, source_target_pairs={{0,64},{64,128},{128,192},{192,0},{1,65},{65,129},{129,193},{193,1... | collective-permute-start | bytes 638984 | tf_op jit(solution)/shard_map/ppermute | solution.py:57
  (24 other events, 28.3 us)
Sparse Core Ops, SparseCore 0:
  10.6 99.1 all-gather.1
